TPU v7x, 32 devices: a whole 2x2x4 slice. The times are simulated.
32 devices in a mesh: parts: 2 (over x), chain: 16 (over z, y, core).
Axes of the slice: x: 2, y: 2, z: 4, core: 2. Of those that a mesh axis runs over, the one named last changes fastest.
Arguments:
- subspace: float32 [64, 8192], P('parts', 'chain'), parts along dimension 0, may hold values from -4 to 4
- s_inv: float32 [8, 32, 2, 256, 256], P('parts', 'chain'), parts along dimension 0, may hold values from -1 to 1
- couple: float32 [32, 512, 256], P('chain', 'parts'), parts along dimension 1, may hold values from -1 to 1
- diag_blocks: float32 [32, 512, 256], P('chain', 'parts'), parts along dimension 1, may hold values from -4 to 4
- weights: float32 [8, 2], P('parts'), parts along dimension 0, may hold values from -1 to 1
Outputs:
- filtered: float32 [64, 8192], P('parts', 'chain'), parts along dimension 0
- applied: float32 [64, 8192], P('parts', 'chain'), parts along dimension 0
- grams: float32 [2, 64, 32], P(None, 'parts'), parts along dimension 1
There are 2 independent parts, one for each index of `parts`. A program takes and returns all parts, laid end to end along the dimension named above; each array names one. Nothing has to cross between parts.
All inputs are finite; a program needn't handle non-finite values.
Results may differ from a plain program's by a relative error of at most 0.00027.
Values sent between devices are 32-bit elements; how exact they have to be, the bound alone decides.
A program may use at most 192 MiB of HBM per device.

v0:
```python
import jax
import jax.numpy as jnp
from jax import lax
from jax.sharding import PartitionSpec as P

highest = lax.Precision.HIGHEST


def passed_along(shard, axis, by):
    peers = lax.axis_size(axis)
    pairs = [(i, i + by) for i in range(peers) if 0 <= i + by < peers]
    return lax.ppermute(shard, axis, pairs)


def inverse_apply(pivot_inv, vecs):
    real_part = jnp.einsum(
        "qnk,qjk->qnj", vecs[:, 0], pivot_inv[:, 0], precision=highest
    ) - jnp.einsum("qnk,qjk->qnj", vecs[:, 1], pivot_inv[:, 1], precision=highest)
    imag_part = jnp.einsum(
        "qnk,qjk->qnj", vecs[:, 0], pivot_inv[:, 1], precision=highest
    ) + jnp.einsum("qnk,qjk->qnj", vecs[:, 1], pivot_inv[:, 0], precision=highest)
    return jnp.stack([real_part, imag_part], axis=1)


def right_apply(vecs, matrix):
    real_part = jnp.einsum(
        "qnk,qkj->qnj", vecs[:, 0], matrix[:, 0], precision=highest
    ) - jnp.einsum("qnk,qkj->qnj", vecs[:, 1], matrix[:, 1], precision=highest)
    imag_part = jnp.einsum(
        "qnk,qkj->qnj", vecs[:, 0], matrix[:, 1], precision=highest
    ) + jnp.einsum("qnk,qkj->qnj", vecs[:, 1], matrix[:, 0], precision=highest)
    return jnp.stack([real_part, imag_part], axis=1)


def couple_down(coupling_blk, vecs):
    return jnp.einsum("qcnk,kj->qcnj", vecs, coupling_blk, precision=highest)


def couple_up(coupling_blk, vecs):
    return jnp.einsum("qcnk,jk->qcnj", vecs, coupling_blk, precision=highest)


def sweep_forward(pivots, couple, start_rows, source, store_all):
    blocks_dev = couple.shape[0]

    def advance(carried, position):
        pivot_inv = lax.dynamic_index_in_dim(pivots, position, 1, keepdims=False)
        coupling_blk = lax.dynamic_index_in_dim(couple, position, 0, keepdims=False)
        combined = carried
        if source is not None:
            rhs_block = lax.dynamic_index_in_dim(source, position, 0, keepdims=False)
            combined = combined.at[:, 0].add(rhs_block[None])
        solved = inverse_apply(pivot_inv, combined)
        return (couple_down(coupling_blk, solved), solved if store_all else None)

    return lax.scan(advance, start_rows, jnp.arange(blocks_dev))


def sweep_backward(pivots, couple, start_rows, solved_all, store_all):
    blocks_dev = couple.shape[0]

    def retreat(carried, position):
        pivot_inv = lax.dynamic_index_in_dim(pivots, position, 1, keepdims=False)
        coupling_blk = lax.dynamic_index_in_dim(couple, position, 0, keepdims=False)
        correction = inverse_apply(pivot_inv, couple_up(coupling_blk, carried))
        if solved_all is not None:
            correction = (
                lax.dynamic_index_in_dim(solved_all, position, 0, keepdims=False) + correction
            )
        return (correction, correction if store_all else None)

    return lax.scan(retreat, start_rows, jnp.arange(blocks_dev), reverse=True)


def shards(subspace, s_inv, couple, diag_blocks, weights):
    points = s_inv.shape[0]
    blocks_dev = couple.shape[0]
    block_width = couple.shape[1]
    vectors = subspace.shape[0]
    source = subspace.reshape(vectors, blocks_dev, block_width).transpose(1, 0, 2)
    zero_rows = jnp.zeros((points, 2, vectors, block_width), jnp.float32)
    plain_eye = jnp.stack(
        [
            jnp.eye(block_width, dtype=jnp.float32),
            jnp.zeros((block_width, block_width), jnp.float32),
        ]
    )
    identity_map = jnp.broadcast_to(plain_eye, (points, 2, block_width, block_width))
    chain_size = lax.axis_size("chain")
    forward_map, _ = sweep_forward(s_inv, couple, identity_map, None, False)
    forward_tip, _ = sweep_forward(s_inv, couple, zero_rows, source, False)

    def forward_hop(hop_index, inbound):
        return passed_along(right_apply(inbound, forward_map) + forward_tip, "chain", 1)

    incoming = lax.fori_loop(0, chain_size - 1, forward_hop, zero_rows)
    _, solved_all = sweep_forward(s_inv, couple, incoming, source, True)
    backward_map, _ = sweep_backward(s_inv, couple, identity_map, None, False)
    backward_tip, _ = sweep_backward(s_inv, couple, zero_rows, solved_all, False)

    def backward_hop(hop_index, inbound):
        return passed_along(right_apply(inbound, backward_map) + backward_tip, "chain", -1)

    outgoing = lax.fori_loop(0, chain_size - 1, backward_hop, zero_rows)
    _, result = sweep_backward(s_inv, couple, outgoing, solved_all, True)
    signed = weights * jnp.array([1.0, -1.0], jnp.float32)
    filtered_blocks = jnp.einsum("rqcnk,qc->rnk", result, signed, precision=highest)
    down_all = jnp.einsum("rnk,rkj->rnj", filtered_blocks, couple, precision=highest)
    from_next = passed_along(filtered_blocks[0], "chain", -1)
    from_prior = passed_along(down_all[-1], "chain", 1)
    diag_term = jnp.einsum("rnk,rjk->rnj", filtered_blocks, diag_blocks, precision=highest)
    upper_rows = jnp.concatenate([filtered_blocks[1:], from_next[None]], axis=0)
    term_up = jnp.einsum("rnk,rjk->rnj", upper_rows, couple, precision=highest)
    lower_rows = jnp.concatenate([from_prior[None], down_all[:-1]], axis=0)
    applied_blocks = diag_term + term_up + lower_rows
    gram_plain = jnp.einsum("rnk,rmk->nm", filtered_blocks, filtered_blocks, precision=highest)
    gram_matrix = jnp.einsum("rnk,rmk->nm", filtered_blocks, applied_blocks, precision=highest)
    summed = lax.psum(jnp.stack([gram_plain, gram_matrix]), "chain")
    grams = summed / (blocks_dev * block_width * chain_size)
    filtered = filtered_blocks.transpose(1, 0, 2).reshape(vectors, blocks_dev * block_width)
    applied = applied_blocks.transpose(1, 0, 2).reshape(vectors, blocks_dev * block_width)
    return (filtered, applied, grams)


def solution(mesh):
    placed = (
        P("parts", "chain"),
        P("parts", "chain", None, None, None),
        P("chain", "parts", None),
        P("chain", "parts", None),
        P("parts", None),
    )
    return jax.shard_map(
        shards,
        mesh=mesh,
        in_specs=placed,
        out_specs=(P("parts", "chain"), P("parts", "chain"), P(None, "parts", None)),
        check_vma=False,
    )
```

profile of v0, /device:TPU:0, one launch (start us, length us, event | category | flops | bytes accessed | tf_op | source)
XLA Modules:
  0.0 591.8 jit_solution(1425416484922783797)
XLA Ops:
  6.5 25.1 %while.104 = (s32[]{:T(128)}, f32[4,2,256,256]{3,2,1,0:T(8,128)S(1)}, s32[2]{0:T(128)S(1)}, f32[4,2,2,256,256]{4,3,0,2,1:T(8,128)}, f32[2,256,256]{2,1,0:T(8,128)S(1)}, /*index=5*/s32[]{:T(128)}, s32[]{:T(128)}, s32[]{:T(128)}) while((s32[]{:T(128)}, f32[4,2,256,256]{3,2,1,0:T(8,128)S(1)}, s32[2]{0:T(128)S(1)}, ...), condition=%wide.region_3.4_spmd, body=%wide.region_2.3_spmd.sunk | while | flops 4832886784 | bytes 23330956 | solution.py:56
  33.3 18.5 %while.105 = (s32[]{:T(128)}, f32[4,2,32,256]{3,2,1,0:T(8,128)S(1)}, s32[2]{0:T(128)S(1)}, f32[2,32,256]{2,1,0:T(8,128)S(1)}, f32[4,2,2,256,256]{4,3,0,2,1:T(8,1...) while((s32[]{:T(128)}, f32[4,2,32,256]{3,2,1,0:T(8,128)S(1)}, s32[2]{0:T(128)S(1)}, ...), condition=%wide.region_5.6_spmd, body=%wide.region_4.5_spmd.sunk | while | flops 604176384 | bytes 10616983 | solution.py:56
  52.6 173.2 %while.106 = (s32[]{:T(128)}, f32[4,2,32,256]{3,2,0,1:T(8,128)S(1)}, f32[4,2,256,256]{3,2,0,1:T(8,128)S(1)}, f32[4,2,32,256]{3,2,0,1:T(8,128)}, s32[]{:T(128)}) while((s32[]{:T(128)}, f32[4,2,32,256]{3,2,0,1:T(8,128)S(1)}, f32[4,2,256,256]{3,2,0,1:T(8,128)S(1)}, f32[4,2,32,256]{3,2,0,1:T(8,128)}, s32[]{:T(128)}) %tuple.236), condition=%wide.region_7.8_spmd, body=%wide.region_6.7_spmd.sunk | while | flops 402849792 | bytes 8388737 | solution.py:96
  167.4 7.4 %collective-permute-start = (f32[4,2,32,256]{3,2,0,1:T(8,128)}, f32[4,2,32,256]{3,2,0,1:T(8,128)S(1)}, u32[]{:S(2)}, u32[]{:S(2)}) collective-permute-start(f32[4,2,32,256]{3,2,0,1:T(8,128)} %maximum_add_fusion.10), channel_id=1, source_target_pairs={{0,1},{1,2},{2,3},{3,4},{4,5},{5,6},{6,7},{7,8},{8,9},{9,10},{10,1... | collective-permute-start | bytes 786440 | tf_op jit(solution)/shard_map/while/body/eval_jaxpr/ppermute | solution.py:12
  225.8 18.2 %while.107 = (s32[]{:T(128)}, f32[4,2,32,256]{3,2,1,0:T(8,128)S(1)}, f32[2,4,2,32,256]{4,3,1,2,0:T(8,128)}, s32[2]{0:T(128)S(1)}, f32[2,32,256]{2,1,0:T(8,128)S(...) while((s32[]{:T(128)}, f32[4,2,32,256]{3,2,1,0:T(8,128)S(1)}, ...), condition=%wide.region_9.10_spmd, body=%wide.region_8.9_spmd.sunk | while | flops 604241920 | bytes 15335643 | solution.py:56
  244.0 19.8 %while.110 = (s32[]{:T(128)}, f32[4,2,32,256]{3,2,0,1:T(8,128)}, s32[2]{0:T(128)S(1)}, f32[2,4,2,32,256]{4,3,1,2,0:T(8,128)}, f32[2,256,256]{2,1,0:T(8,128)S(1)}...) while((s32[]{:T(128)}, f32[4,2,32,256]{3,2,0,1:T(8,128)}, ...), condition=%wide.region_11.12_spmd.clone, body=%wide.region_10.11_spmd.clone.sunk | while | flops 604241920 | bytes 13369545 | solution.py:72
  265.0 27.5 %while.103 = (s32[]{:T(128)}, f32[4,2,256,256]{3,2,0,1:T(8,128)S(1)}, s32[2]{0:T(128)S(1)}, f32[2,256,256]{2,1,0:T(8,128)S(1)}, f32[4,2,2,256,256]{4,3,0,2,1:T(8,128)}, /*index=5*/s32[]{:T(128)}, s32[]{:T(128)}, s32[]{:T(128)}) while((s32[]{:T(128)}, f32[4,2,256,256]{3,2,0,1:T(8,128)S(1)}, s32[2]{0:T(128)S(1)}, f32[2,256,256]{2,1,0:T(8,128)S(1)}, ...), condition=%wide.region_1.2_spmd, body=%wide.region_0.1_spmd.sunk | while | flops 4832886784 | bytes 27525272 | solution.py:72
  292.6 201.3 %while.108 = (s32[]{:T(128)}, f32[4,2,32,256]{3,2,0,1:T(8,128)S(1)}, f32[4,2,256,256]{3,2,0,1:T(8,128)S(1)}, f32[4,2,32,256]{3,2,0,1:T(8,128)}, s32[]{:T(128)}) while((s32[]{:T(128)}, f32[4,2,32,256]{3,2,0,1:T(8,128)S(1)}, f32[4,2,256,256]{3,2,0,1:T(8,128)S(1)}, f32[4,2,32,256]{3,2,0,1:T(8,128)}, s32[]{:T(128)}) %tuple.225), condition=%wide.region_13.14_spmd, body=%wide.region_12.13_spmd.sunk | while | flops 402849792 | bytes 7340133 | solution.py:104
  311.9 8.1 %collective-permute-done.1 = f32[4,2,32,256]{3,2,0,1:T(8,128)S(1)} collective-permute-done((f32[4,2,32,256]{3,2,0,1:T(8,128)}, f32[4,2,32,256]{3,2,0,1:T(8,128)S(1)}, u32[]{:S(2)}, u32[]{:S(2)}) %collective-permute-start.1) | collective-permute-done | bytes 262176 | tf_op jit(solution)/shard_map/while/body/eval_jaxpr/ppermute | solution.py:12
  339.1 8.1 %collective-permute-done.1 = f32[4,2,32,256]{3,2,0,1:T(8,128)S(1)} collective-permute-done((f32[4,2,32,256]{3,2,0,1:T(8,128)}, f32[4,2,32,256]{3,2,0,1:T(8,128)S(1)}, u32[]{:S(2)}, u32[]{:S(2)}) %collective-permute-start.1) | collective-permute-done | bytes 262176 | tf_op jit(solution)/shard_map/while/body/eval_jaxpr/ppermute | solution.py:12
  353.1 7.5 %collective-permute-done.1 = f32[4,2,32,256]{3,2,0,1:T(8,128)S(1)} collective-permute-done((f32[4,2,32,256]{3,2,0,1:T(8,128)}, f32[4,2,32,256]{3,2,0,1:T(8,128)S(1)}, u32[]{:S(2)}, u32[]{:S(2)}) %collective-permute-start.1) | collective-permute-done | bytes 262176 | tf_op jit(solution)/shard_map/while/body/eval_jaxpr/ppermute | solution.py:12
  366.4 7.5 %collective-permute-done.1 = f32[4,2,32,256]{3,2,0,1:T(8,128)S(1)} collective-permute-done((f32[4,2,32,256]{3,2,0,1:T(8,128)}, f32[4,2,32,256]{3,2,0,1:T(8,128)S(1)}, u32[]{:S(2)}, u32[]{:S(2)}) %collective-permute-start.1) | collective-permute-done | bytes 262176 | tf_op jit(solution)/shard_map/while/body/eval_jaxpr/ppermute | solution.py:12
  379.7 7.5 %collective-permute-done.1 = f32[4,2,32,256]{3,2,0,1:T(8,128)S(1)} collective-permute-done((f32[4,2,32,256]{3,2,0,1:T(8,128)}, f32[4,2,32,256]{3,2,0,1:T(8,128)S(1)}, u32[]{:S(2)}, u32[]{:S(2)}) %collective-permute-start.1) | collective-permute-done | bytes 262176 | tf_op jit(solution)/shard_map/while/body/eval_jaxpr/ppermute | solution.py:12
  393.1 7.5 %collective-permute-done.1 = f32[4,2,32,256]{3,2,0,1:T(8,128)S(1)} collective-permute-done((f32[4,2,32,256]{3,2,0,1:T(8,128)}, f32[4,2,32,256]{3,2,0,1:T(8,128)S(1)}, u32[]{:S(2)}, u32[]{:S(2)}) %collective-permute-start.1) | collective-permute-done | bytes 262176 | tf_op jit(solution)/shard_map/while/body/eval_jaxpr/ppermute | solution.py:12
  406.4 7.5 %collective-permute-done.1 = f32[4,2,32,256]{3,2,0,1:T(8,128)S(1)} collective-permute-done((f32[4,2,32,256]{3,2,0,1:T(8,128)}, f32[4,2,32,256]{3,2,0,1:T(8,128)S(1)}, u32[]{:S(2)}, u32[]{:S(2)}) %collective-permute-start.1) | collective-permute-done | bytes 262176 | tf_op jit(solution)/shard_map/while/body/eval_jaxpr/ppermute | solution.py:12
  419.7 7.5 %collective-permute-done.1 = f32[4,2,32,256]{3,2,0,1:T(8,128)S(1)} collective-permute-done((f32[4,2,32,256]{3,2,0,1:T(8,128)}, f32[4,2,32,256]{3,2,0,1:T(8,128)S(1)}, u32[]{:S(2)}, u32[]{:S(2)}) %collective-permute-start.1) | collective-permute-done | bytes 262176 | tf_op jit(solution)/shard_map/while/body/eval_jaxpr/ppermute | solution.py:12
  433.1 7.5 %collective-permute-done.1 = f32[4,2,32,256]{3,2,0,1:T(8,128)S(1)} collective-permute-done((f32[4,2,32,256]{3,2,0,1:T(8,128)}, f32[4,2,32,256]{3,2,0,1:T(8,128)S(1)}, u32[]{:S(2)}, u32[]{:S(2)}) %collective-permute-start.1) | collective-permute-done | bytes 262176 | tf_op jit(solution)/shard_map/while/body/eval_jaxpr/ppermute | solution.py:12
  446.4 7.5 %collective-permute-done.1 = f32[4,2,32,256]{3,2,0,1:T(8,128)S(1)} collective-permute-done((f32[4,2,32,256]{3,2,0,1:T(8,128)}, f32[4,2,32,256]{3,2,0,1:T(8,128)S(1)}, u32[]{:S(2)}, u32[]{:S(2)}) %collective-permute-start.1) | collective-permute-done | bytes 262176 | tf_op jit(solution)/shard_map/while/body/eval_jaxpr/ppermute | solution.py:12
  459.8 7.5 %collective-permute-done.1 = f32[4,2,32,256]{3,2,0,1:T(8,128)S(1)} collective-permute-done((f32[4,2,32,256]{3,2,0,1:T(8,128)}, f32[4,2,32,256]{3,2,0,1:T(8,128)S(1)}, u32[]{:S(2)}, u32[]{:S(2)}) %collective-permute-start.1) | collective-permute-done | bytes 262176 | tf_op jit(solution)/shard_map/while/body/eval_jaxpr/ppermute | solution.py:12
  473.1 7.5 %collective-permute-done.1 = f32[4,2,32,256]{3,2,0,1:T(8,128)S(1)} collective-permute-done((f32[4,2,32,256]{3,2,0,1:T(8,128)}, f32[4,2,32,256]{3,2,0,1:T(8,128)S(1)}, u32[]{:S(2)}, u32[]{:S(2)}) %collective-permute-start.1) | collective-permute-done | bytes 262176 | tf_op jit(solution)/shard_map/while/body/eval_jaxpr/ppermute | solution.py:12
  486.4 7.5 %collective-permute-done.1 = f32[4,2,32,256]{3,2,0,1:T(8,128)S(1)} collective-permute-done((f32[4,2,32,256]{3,2,0,1:T(8,128)}, f32[4,2,32,256]{3,2,0,1:T(8,128)S(1)}, u32[]{:S(2)}, u32[]{:S(2)}) %collective-permute-start.1) | collective-permute-done | bytes 262176 | tf_op jit(solution)/shard_map/while/body/eval_jaxpr/ppermute | solution.py:12
  494.0 18.5 %while.109 = (s32[]{:T(128)}, f32[4,2,32,256]{3,2,0,1:T(8,128)S(1)}, f32[2,4,2,32,256]{4,1,2,3,0:T(4,128)S(1)}, s32[2]{0:T(128)S(1)}, f32[2,4,2,32,256]{4,3,1,2,...) while((s32[]{:T(128)}, f32[4,2,32,256]{3,2,0,1:T(8,128)S(1)}, ...), condition=%wide.region_15.16_spmd, body=%wide.region_14.15_spmd.sunk | while | flops 604307456 | bytes 14680271 | solution.py:72
  515.0 8.2 %collective-permute-start.3 = (f32[32,256]{1,0:T(8,128)S(1)}, f32[32,256]{1,0:T(8,128)S(1)}, u32[]{:S(2)}, u32[]{:S(2)}) collective-permute-start(f32[32,256]{1,0:T(8,128)S(1)} %get-tuple-element.827), channel_id=1, source_target_pairs={{0,1},{1,2},{2,3},{3,4},{4,5},{5,6},{6,7},{7,8},{8,9},{9,10},{10,1... | collective-permute-start | bytes 98312 | tf_op jit(solution)/shard_map/ppermute | solution.py:12
  525.4 64.7 %psum.7 = f32[2,32,32]{2,1,0:T(8,128)S(1)} all-reduce(f32[2,32,32]{2,1,0:T(8,128)S(1)} %pad_maximum_fusion.4), channel_id=1, replica_groups=mesh['parts'=2,'chain'=16] {'chain'}, use_global_device_ids=true, to_apply=%region_16.17 | all-reduce | flops 2048 | bytes 16384 | tf_op jit(solution)/shard_map/psum | solution.py:118
  (395 shorter events, 386.5 us)
Async XLA Ops:
  63.6 8.1 %collective-permute-start = (f32[4,2,32,256]{3,2,0,1:T(8,128)}, f32[4,2,32,256]{3,2,0,1:T(8,128)S(1)}, u32[]{:S(2)}, u32[]{:S(2)}) collective-permute-start(f32[4,2,32,256]{3,2,0,1:T(8,128)} %maximum_add_fusion.10), channel_id=1, source_target_pairs={{0,1},{1,2},{2,3},{3,4},{4,5},{5,6},{6,7},{7,8},{8,9},{9,10},{10,1... | collective-permute-start | bytes 786440 | tf_op jit(solution)/shard_map/while/body/eval_jaxpr/ppermute | solution.py:12
  155.8 7.9 %collective-permute-start = (f32[4,2,32,256]{3,2,0,1:T(8,128)}, f32[4,2,32,256]{3,2,0,1:T(8,128)S(1)}, u32[]{:S(2)}, u32[]{:S(2)}) collective-permute-start(f32[4,2,32,256]{3,2,0,1:T(8,128)} %maximum_add_fusion.10), channel_id=1, source_target_pairs={{0,1},{1,2},{2,3},{3,4},{4,5},{5,6},{6,7},{7,8},{8,9},{9,10},{10,1... | collective-permute-start | bytes 786440 | tf_op jit(solution)/shard_map/while/body/eval_jaxpr/ppermute | solution.py:12
  167.4 8.8 %collective-permute-start = (f32[4,2,32,256]{3,2,0,1:T(8,128)}, f32[4,2,32,256]{3,2,0,1:T(8,128)S(1)}, u32[]{:S(2)}, u32[]{:S(2)}) collective-permute-start(f32[4,2,32,256]{3,2,0,1:T(8,128)} %maximum_add_fusion.10), channel_id=1, source_target_pairs={{0,1},{1,2},{2,3},{3,4},{4,5},{5,6},{6,7},{7,8},{8,9},{9,10},{10,1... | collective-permute-start | bytes 786440 | tf_op jit(solution)/shard_map/while/body/eval_jaxpr/ppermute | solution.py:12
  179.8 8.8 %collective-permute-start = (f32[4,2,32,256]{3,2,0,1:T(8,128)}, f32[4,2,32,256]{3,2,0,1:T(8,128)S(1)}, u32[]{:S(2)}, u32[]{:S(2)}) collective-permute-start(f32[4,2,32,256]{3,2,0,1:T(8,128)} %maximum_add_fusion.10), channel_id=1, source_target_pairs={{0,1},{1,2},{2,3},{3,4},{4,5},{5,6},{6,7},{7,8},{8,9},{9,10},{10,1... | collective-permute-start | bytes 786440 | tf_op jit(solution)/shard_map/while/body/eval_jaxpr/ppermute | solution.py:12
  192.2 8.8 %collective-permute-start = (f32[4,2,32,256]{3,2,0,1:T(8,128)}, f32[4,2,32,256]{3,2,0,1:T(8,128)S(1)}, u32[]{:S(2)}, u32[]{:S(2)}) collective-permute-start(f32[4,2,32,256]{3,2,0,1:T(8,128)} %maximum_add_fusion.10), channel_id=1, source_target_pairs={{0,1},{1,2},{2,3},{3,4},{4,5},{5,6},{6,7},{7,8},{8,9},{9,10},{10,1... | collective-permute-start | bytes 786440 | tf_op jit(solution)/shard_map/while/body/eval_jaxpr/ppermute | solution.py:12
  204.6 8.8 %collective-permute-start = (f32[4,2,32,256]{3,2,0,1:T(8,128)}, f32[4,2,32,256]{3,2,0,1:T(8,128)S(1)}, u32[]{:S(2)}, u32[]{:S(2)}) collective-permute-start(f32[4,2,32,256]{3,2,0,1:T(8,128)} %maximum_add_fusion.10), channel_id=1, source_target_pairs={{0,1},{1,2},{2,3},{3,4},{4,5},{5,6},{6,7},{7,8},{8,9},{9,10},{10,1... | collective-permute-start | bytes 786440 | tf_op jit(solution)/shard_map/while/body/eval_jaxpr/ppermute | solution.py:12
  217.0 8.8 %collective-permute-start = (f32[4,2,32,256]{3,2,0,1:T(8,128)}, f32[4,2,32,256]{3,2,0,1:T(8,128)S(1)}, u32[]{:S(2)}, u32[]{:S(2)}) collective-permute-start(f32[4,2,32,256]{3,2,0,1:T(8,128)} %maximum_add_fusion.10), channel_id=1, source_target_pairs={{0,1},{1,2},{2,3},{3,4},{4,5},{5,6},{6,7},{7,8},{8,9},{9,10},{10,1... | collective-permute-start | bytes 786440 | tf_op jit(solution)/shard_map/while/body/eval_jaxpr/ppermute | solution.py:12
  297.4 8.7 %collective-permute-start.1 = (f32[4,2,32,256]{3,2,0,1:T(8,128)}, f32[4,2,32,256]{3,2,0,1:T(8,128)S(1)}, u32[]{:S(2)}, u32[]{:S(2)}) collective-permute-start(f32[4,2,32,256]{3,2,0,1:T(8,128)} %maximum_add_fusion.11), channel_id=1, source_target_pairs={{1,0},{2,1},{3,2},{4,3},{5,4},{6,5},{7,6},{8,7},{9,8},{10,9},{11,1... | collective-permute-start | bytes 786440 | tf_op jit(solution)/shard_map/while/body/eval_jaxpr/ppermute | solution.py:12
  310.6 9.4 %collective-permute-start.1 = (f32[4,2,32,256]{3,2,0,1:T(8,128)}, f32[4,2,32,256]{3,2,0,1:T(8,128)S(1)}, u32[]{:S(2)}, u32[]{:S(2)}) collective-permute-start(f32[4,2,32,256]{3,2,0,1:T(8,128)} %maximum_add_fusion.11), channel_id=1, source_target_pairs={{1,0},{2,1},{3,2},{4,3},{5,4},{6,5},{7,6},{8,7},{9,8},{10,9},{11,1... | collective-permute-start | bytes 786440 | tf_op jit(solution)/shard_map/while/body/eval_jaxpr/ppermute | solution.py:12
  324.6 8.7 %collective-permute-start.1 = (f32[4,2,32,256]{3,2,0,1:T(8,128)}, f32[4,2,32,256]{3,2,0,1:T(8,128)S(1)}, u32[]{:S(2)}, u32[]{:S(2)}) collective-permute-start(f32[4,2,32,256]{3,2,0,1:T(8,128)} %maximum_add_fusion.11), channel_id=1, source_target_pairs={{1,0},{2,1},{3,2},{4,3},{5,4},{6,5},{7,6},{8,7},{9,8},{10,9},{11,1... | collective-permute-start | bytes 786440 | tf_op jit(solution)/shard_map/while/body/eval_jaxpr/ppermute | solution.py:12
  337.8 9.4 %collective-permute-start.1 = (f32[4,2,32,256]{3,2,0,1:T(8,128)}, f32[4,2,32,256]{3,2,0,1:T(8,128)S(1)}, u32[]{:S(2)}, u32[]{:S(2)}) collective-permute-start(f32[4,2,32,256]{3,2,0,1:T(8,128)} %maximum_add_fusion.11), channel_id=1, source_target_pairs={{1,0},{2,1},{3,2},{4,3},{5,4},{6,5},{7,6},{8,7},{9,8},{10,9},{11,1... | collective-permute-start | bytes 786440 | tf_op jit(solution)/shard_map/while/body/eval_jaxpr/ppermute | solution.py:12
  351.8 8.8 %collective-permute-start.1 = (f32[4,2,32,256]{3,2,0,1:T(8,128)}, f32[4,2,32,256]{3,2,0,1:T(8,128)S(1)}, u32[]{:S(2)}, u32[]{:S(2)}) collective-permute-start(f32[4,2,32,256]{3,2,0,1:T(8,128)} %maximum_add_fusion.11), channel_id=1, source_target_pairs={{1,0},{2,1},{3,2},{4,3},{5,4},{6,5},{7,6},{8,7},{9,8},{10,9},{11,1... | collective-permute-start | bytes 786440 | tf_op jit(solution)/shard_map/while/body/eval_jaxpr/ppermute | solution.py:12
  365.1 8.8 %collective-permute-start.1 = (f32[4,2,32,256]{3,2,0,1:T(8,128)}, f32[4,2,32,256]{3,2,0,1:T(8,128)S(1)}, u32[]{:S(2)}, u32[]{:S(2)}) collective-permute-start(f32[4,2,32,256]{3,2,0,1:T(8,128)} %maximum_add_fusion.11), channel_id=1, source_target_pairs={{1,0},{2,1},{3,2},{4,3},{5,4},{6,5},{7,6},{8,7},{9,8},{10,9},{11,1... | collective-permute-start | bytes 786440 | tf_op jit(solution)/shard_map/while/body/eval_jaxpr/ppermute | solution.py:12
  378.5 8.8 %collective-permute-start.1 = (f32[4,2,32,256]{3,2,0,1:T(8,128)}, f32[4,2,32,256]{3,2,0,1:T(8,128)S(1)}, u32[]{:S(2)}, u32[]{:S(2)}) collective-permute-start(f32[4,2,32,256]{3,2,0,1:T(8,128)} %maximum_add_fusion.11), channel_id=1, source_target_pairs={{1,0},{2,1},{3,2},{4,3},{5,4},{6,5},{7,6},{8,7},{9,8},{10,9},{11,1... | collective-permute-start | bytes 786440 | tf_op jit(solution)/shard_map/while/body/eval_jaxpr/ppermute | solution.py:12
  391.8 8.8 %collective-permute-start.1 = (f32[4,2,32,256]{3,2,0,1:T(8,128)}, f32[4,2,32,256]{3,2,0,1:T(8,128)S(1)}, u32[]{:S(2)}, u32[]{:S(2)}) collective-permute-start(f32[4,2,32,256]{3,2,0,1:T(8,128)} %maximum_add_fusion.11), channel_id=1, source_target_pairs={{1,0},{2,1},{3,2},{4,3},{5,4},{6,5},{7,6},{8,7},{9,8},{10,9},{11,1... | collective-permute-start | bytes 786440 | tf_op jit(solution)/shard_map/while/body/eval_jaxpr/ppermute | solution.py:12
  405.1 8.8 %collective-permute-start.1 = (f32[4,2,32,256]{3,2,0,1:T(8,128)}, f32[4,2,32,256]{3,2,0,1:T(8,128)S(1)}, u32[]{:S(2)}, u32[]{:S(2)}) collective-permute-start(f32[4,2,32,256]{3,2,0,1:T(8,128)} %maximum_add_fusion.11), channel_id=1, source_target_pairs={{1,0},{2,1},{3,2},{4,3},{5,4},{6,5},{7,6},{8,7},{9,8},{10,9},{11,1... | collective-permute-start | bytes 786440 | tf_op jit(solution)/shard_map/while/body/eval_jaxpr/ppermute | solution.py:12
  418.5 8.8 %collective-permute-start.1 = (f32[4,2,32,256]{3,2,0,1:T(8,128)}, f32[4,2,32,256]{3,2,0,1:T(8,128)S(1)}, u32[]{:S(2)}, u32[]{:S(2)}) collective-permute-start(f32[4,2,32,256]{3,2,0,1:T(8,128)} %maximum_add_fusion.11), channel_id=1, source_target_pairs={{1,0},{2,1},{3,2},{4,3},{5,4},{6,5},{7,6},{8,7},{9,8},{10,9},{11,1... | collective-permute-start | bytes 786440 | tf_op jit(solution)/shard_map/while/body/eval_jaxpr/ppermute | solution.py:12
  431.8 8.8 %collective-permute-start.1 = (f32[4,2,32,256]{3,2,0,1:T(8,128)}, f32[4,2,32,256]{3,2,0,1:T(8,128)S(1)}, u32[]{:S(2)}, u32[]{:S(2)}) collective-permute-start(f32[4,2,32,256]{3,2,0,1:T(8,128)} %maximum_add_fusion.11), channel_id=1, source_target_pairs={{1,0},{2,1},{3,2},{4,3},{5,4},{6,5},{7,6},{8,7},{9,8},{10,9},{11,1... | collective-permute-start | bytes 786440 | tf_op jit(solution)/shard_map/while/body/eval_jaxpr/ppermute | solution.py:12
  445.1 8.8 %collective-permute-start.1 = (f32[4,2,32,256]{3,2,0,1:T(8,128)}, f32[4,2,32,256]{3,2,0,1:T(8,128)S(1)}, u32[]{:S(2)}, u32[]{:S(2)}) collective-permute-start(f32[4,2,32,256]{3,2,0,1:T(8,128)} %maximum_add_fusion.11), channel_id=1, source_target_pairs={{1,0},{2,1},{3,2},{4,3},{5,4},{6,5},{7,6},{8,7},{9,8},{10,9},{11,1... | collective-permute-start | bytes 786440 | tf_op jit(solution)/shard_map/while/body/eval_jaxpr/ppermute | solution.py:12
  458.5 8.8 %collective-permute-start.1 = (f32[4,2,32,256]{3,2,0,1:T(8,128)}, f32[4,2,32,256]{3,2,0,1:T(8,128)S(1)}, u32[]{:S(2)}, u32[]{:S(2)}) collective-permute-start(f32[4,2,32,256]{3,2,0,1:T(8,128)} %maximum_add_fusion.11), channel_id=1, source_target_pairs={{1,0},{2,1},{3,2},{4,3},{5,4},{6,5},{7,6},{8,7},{9,8},{10,9},{11,1... | collective-permute-start | bytes 786440 | tf_op jit(solution)/shard_map/while/body/eval_jaxpr/ppermute | solution.py:12
  471.8 8.8 %collective-permute-start.1 = (f32[4,2,32,256]{3,2,0,1:T(8,128)}, f32[4,2,32,256]{3,2,0,1:T(8,128)S(1)}, u32[]{:S(2)}, u32[]{:S(2)}) collective-permute-start(f32[4,2,32,256]{3,2,0,1:T(8,128)} %maximum_add_fusion.11), channel_id=1, source_target_pairs={{1,0},{2,1},{3,2},{4,3},{5,4},{6,5},{7,6},{8,7},{9,8},{10,9},{11,1... | collective-permute-start | bytes 786440 | tf_op jit(solution)/shard_map/while/body/eval_jaxpr/ppermute | solution.py:12
  485.1 8.8 %collective-permute-start.1 = (f32[4,2,32,256]{3,2,0,1:T(8,128)}, f32[4,2,32,256]{3,2,0,1:T(8,128)S(1)}, u32[]{:S(2)}, u32[]{:S(2)}) collective-permute-start(f32[4,2,32,256]{3,2,0,1:T(8,128)} %maximum_add_fusion.11), channel_id=1, source_target_pairs={{1,0},{2,1},{3,2},{4,3},{5,4},{6,5},{7,6},{8,7},{9,8},{10,9},{11,1... | collective-permute-start | bytes 786440 | tf_op jit(solution)/shard_map/while/body/eval_jaxpr/ppermute | solution.py:12
  513.3 11.3 %collective-permute-start.2 = (f32[32,256]{1,0:T(8,128)S(1)}, f32[32,256]{1,0:T(8,128)S(1)}, u32[]{:S(2)}, u32[]{:S(2)}) collective-permute-start(f32[32,256]{1,0:T(8,128)S(1)} %get-tuple-element.830), channel_id=1, source_target_pairs={{1,0},{2,1},{3,2},{4,3},{5,4},{6,5},{7,6},{8,7},{9,8},{10,9},{11,1... | collective-permute-start | bytes 98312 | tf_op jit(solution)/shard_map/ppermute | solution.py:12
  515.0 9.6 %collective-permute-start.3 = (f32[32,256]{1,0:T(8,128)S(1)}, f32[32,256]{1,0:T(8,128)S(1)}, u32[]{:S(2)}, u32[]{:S(2)}) collective-permute-start(f32[32,256]{1,0:T(8,128)S(1)} %get-tuple-element.827), channel_id=1, source_target_pairs={{0,1},{1,2},{2,3},{3,4},{4,5},{5,6},{6,7},{7,8},{8,9},{9,10},{10,1... | collective-permute-start | bytes 98312 | tf_op jit(solution)/shard_map/ppermute | solution.py:12
  (38 other events, 694.5 us)
where the time goes:
time: 601 us; the launch traced here: 592 us
  matrix products  161 us (27%)
  waiting for transfers between devices  134 us (22%)
  starting transfers between devices  127 us (21%)
  blocking collectives  64.7 us (11%)
  local copies, waits for them, and re-layouts  39.9 us (7%)
  other arithmetic  39.4 us (7%)
  loops' own time  24.9 us (4%)
    ppermute x32, waiting for transfers between devices, passed_along(): return lax.ppermute(shard, axis, pairs)  134 us
    ppermute x32, starting transfers between devices, passed_along(): return lax.ppermute(shard, axis, pairs)  127 us
    psum x1, blocking collectives, shards(): summed = lax.psum(jnp.stack([gram_plain, gram_matrix]), 'chain')  64.7 us
    add x15, other arithmetic, backward_hop(): right_apply(inbound, backward_map) + backward_tip  25.5 us
    dot_general x30, matrix products, right_apply(): jnp.einsum('qnk,qkj->qnj', vecs[:, 1], matrix[:, 0], precision=highest)  21.1 us
    dot_general x30, matrix products, right_apply(): jnp.einsum('qnk,qkj->qnj', vecs[:, 1], matrix[:, 1], precision=highest)  21.1 us
    dot_general x30, matrix products, right_apply(): jnp.einsum('qnk,qkj->qnj', vecs[:, 0], matrix[:, 0], precision=highest)  21.1 us
    dot_general x30, matrix products, right_apply(): jnp.einsum('qnk,qkj->qnj', vecs[:, 0], matrix[:, 1], precision=highest)  21.1 us
  transfers between devices with their start and end apart: 32, of which 30 were waited for; matrix products, arithmetic and copies ran while one was open for 0% of the time, Pallas kernels for 0%

commit v1 on v0

v1 whole, which is shorter than its diff:
```python
import functools

import jax
import jax.numpy as jnp
from jax import lax
from jax.experimental import pallas as pl
from jax.experimental.pallas import tpu as pltpu
from jax.sharding import PartitionSpec as P

MESH = pl.DeviceIdType.MESH
f32, bf16 = jnp.float32, jnp.bfloat16
NT = (((1,), (1,)), ((), ()))
NN = (((1,), (0,)), ((), ()))


def split(a):
    high = a.astype(bf16)
    return high, (a - high.astype(f32)).astype(bf16)


def dot(a, b, dims):
    return lax.dot_general(a, b, dims, preferred_element_type=f32)


def product(a, b, dims):
    return dot(a[0], b[0], dims) + (dot(a[0], b[1], dims) + dot(a[1], b[0], dims))


def apply_map(rows, high, low):
    half, width = rows.shape[0] // 2, rows.shape[1]
    rows_high, rows_low = split(rows)
    both = dot(jnp.concatenate([rows_high, rows_low], axis=0), high, NT)
    mixed = both[: 2 * half] + (both[2 * half :] + dot(rows_high, low, NT))
    results = []
    for at in range(0, mixed.shape[1], 2 * width):
        by_re, by_im = mixed[:, at : at + width], mixed[:, at + width : at + 2 * width]
        results.append(
            jnp.concatenate([by_re[:half] - by_im[half:], by_re[half:] + by_im[:half]], axis=0)
        )
    return results


def compose(a, b):
    width = b[0].shape[1]
    by_re = product(a, (b[0][:width], b[1][:width]), NN)
    by_im = product(a, (b[0][width:], b[1][width:]), NN)
    return jnp.concatenate([by_re[:width] - by_im[width:], by_im[:width] + by_re[width:]], axis=0)


def kernel(
    n, f_hbm, s_hbm, e_hbm, d_hbm, w_ref, filt_ref, app_ref, gram_ref,
    F, S, E, D, Eh, El, Th, Tl, Wh, Wl, Nh, Nl, Ch, Cl, Rh, Rl,
    tip, cin, cout, y, u, xin, xout, pf, pfin, ff, fnext, fsend, down, downin,
    gown, gin, gsib, gfin, local_sem, swap_send, swap_recv, fwd_send, fwd_recv,
    bwd_send, bwd_recv, one_send, one_recv, all_send, all_recv,
):
    me = lax.axis_index("chain")
    chip, core = lax.div(me, 2), lax.rem(me, 2)
    sib = chip * 2 + 1 - core
    after = jnp.minimum(chip + 1, n - 1) * 2 + core
    before = jnp.maximum(chip - 1, 0) * 2 + core
    right = jnp.minimum(me + 1, 2 * n - 1)
    left = jnp.maximum(me - 1, 0)
    first, last = chip == 0, chip == n - 1
    points, blocks = S.shape[0], S.shape[1]
    mine = e_hbm.shape[0]
    width = e_hbm.shape[1]
    vectors = f_hbm.shape[0]

    def greet(device):
        pl.semaphore_signal(barrier, inc=1, device_id={"chain": device}, device_id_type=MESH)

    def remote(src, dst, send, recv, device):
        return pltpu.make_async_remote_copy(
            src_ref=src, dst_ref=dst, send_sem=send, recv_sem=recv,
            device_id={"chain": device}, device_id_type=MESH,
        )

    here = pl.ds(core * mine, mine)
    own_points = pl.ds(core * points, points)
    sib_points = pl.ds((1 - core) * points, points)
    local = [
        pltpu.make_async_copy(f_hbm, F.at[core], local_sem.at[0]),
        pltpu.make_async_copy(e_hbm, E.at[here], local_sem.at[1]),
        pltpu.make_async_copy(s_hbm.at[own_points], S.at[:, here], local_sem.at[2]),
        pltpu.make_async_copy(d_hbm, D, local_sem.at[3]),
    ]
    for copy in local:
        copy.start()

    barrier = pltpu.get_barrier_semaphore()
    greet(sib)

    @pl.when(jnp.logical_not(first))
    def _():
        greet(before)
        greet(core)

    @pl.when(jnp.logical_not(last))
    def _():
        greet(after)

    @pl.when(jnp.logical_and(core == 0, jnp.logical_not(first)))
    def _():
        greet(left)

    @pl.when(jnp.logical_and(core == 1, jnp.logical_not(last)))
    def _():
        greet(right)

    has_next = jnp.where(last, 0, 1)
    has_prev = jnp.where(first, 0, 1)
    pl.semaphore_wait(
        barrier,
        1 + has_next + has_prev + jnp.where(core == 1, has_next, has_prev)
        + jnp.where(first, n - 1, 0),
    )
    swap = [
        remote(f_hbm, F.at[core], swap_send.at[0], swap_recv.at[0], sib),
        remote(e_hbm, E.at[here], swap_send.at[1], swap_recv.at[1], sib),
        remote(s_hbm.at[sib_points], S.at[:, here], swap_send.at[2], swap_recv.at[2], sib),
    ]
    for copy in swap:
        copy.start()
    for copy in local:
        copy.wait()
    for copy in swap:
        copy.wait()

    @pl.loop(0, blocks)
    def _(b):
        Eh[b], El[b] = split(E[b])
        Th[b], Tl[b] = split(E[b].T)

    @pl.loop(0, points)
    def _(q):
        @pl.loop(0, blocks)
        def _(b):
            high, low = split(S[q, b])
            Wh[q, b, : 2 * width], Wl[q, b, : 2 * width] = high, low
            turned = (Th[b], Tl[b])
            for part in range(2):
                rows = slice(part * width, (part + 1) * width)
                out = split(product(turned, (high[rows], low[rows]), NN))
                to = slice((2 + part) * width, (3 + part) * width)
                Wh[q, b, to], Wl[q, b, to] = out

    def source(b):
        rows = F[b // mine, :, (b % mine) * width : (b % mine + 1) * width]
        return jnp.concatenate([rows, jnp.zeros_like(rows)], axis=0)

    low_rows = slice(2 * width, 4 * width)
    carried = [None] * points
    for b in range(blocks):
        for q in range(points):
            z = source(b) if b == 0 else source(b) + carried[q]
            (carried[q],) = apply_map(z, Wh[q, b, low_rows], Wl[q, b, low_rows])
    for q in range(points):
        tip[q] = carried[q]

    @pl.when(jnp.logical_and(jnp.logical_not(first), jnp.logical_not(last)))
    def _():
        @pl.loop(0, points)
        def _(q):
            Ch[q], Cl[q] = Wh[q, 0, low_rows], Wl[q, 0, low_rows]

            @pl.loop(1, blocks)
            def _(b):
                Ch[q], Cl[q] = split(
                    compose((Wh[q, b, low_rows], Wl[q, b, low_rows]), (Ch[q], Cl[q]))
                )

    forward = [
        remote(cout.at[q], cin.at[q], fwd_send.at[q], fwd_recv.at[q], after) for q in range(points)
    ]
    backward = [
        remote(xout.at[q], xin.at[q], bwd_send.at[q], bwd_recv.at[q], before)
        for q in range(points)
    ]

    def sweep_forward():
        @pl.when(first)
        def _():
            for q in range(points):
                cout[q] = tip[q]
                forward[q].start()
            cin[...] = jnp.zeros_like(cin)

        @pl.when(jnp.logical_not(first))
        def _():
            for q in range(points):
                forward[q].wait_recv()

                @pl.when(jnp.logical_not(last))
                def _():
                    cout[q] = tip[q] + apply_map(cin[q], Ch[q], Cl[q])[0]
                    forward[q].start()

        entering = [cin[q] for q in range(points)]
        for b in range(blocks):
            for q in range(points):
                z = source(b) + entering[q]
                y[q, b], entering[q] = apply_map(z, Wh[q, b], Wl[q, b])

    def backward_maps():
        @pl.loop(0, points)
        def _(q):
            @pl.loop(0, blocks)
            def _(b):
                pivot = (Wh[q, b, : 2 * width], Wl[q, b, : 2 * width])
                Nh[q, b], Nl[q, b] = split(product(pivot, (Eh[b], El[b]), NN))

            @pl.when(jnp.logical_not(last))
            def _():
                Rh[q, blocks - 1], Rl[q, blocks - 1] = Nh[q, blocks - 1], Nl[q, blocks - 1]

                @pl.loop(1, blocks)
                def _(step):
                    b = blocks - 1 - step
                    Rh[q, b], Rl[q, b] = split(
                        compose((Nh[q, b], Nl[q, b]), (Rh[q, b + 1], Rl[q, b + 1]))
                    )

    maps_first = chip * 2 >= n

    @pl.loop(0, 3)
    def _(step):
        @pl.when(step == 1)
        def _():
            sweep_forward()

        @pl.when(step == jnp.where(maps_first, 0, 2))
        def _():
            backward_maps()

    carried = [None] * points
    for b in reversed(range(blocks)):
        for q in range(points):
            if b == blocks - 1:
                carried[q] = y[q, b]
            else:
                carried[q] = y[q, b] + apply_map(carried[q], Nh[q, b], Nl[q, b])[0]
            u[q, b] = carried[q]

    weight_re = [w_ref[core * points + q, 0] for q in range(points)]
    weight_im = [w_ref[core * points + q, 1] for q in range(points)]

    def filtered_part(q, x):
        return weight_re[q] * x[:vectors] - weight_im[q] * x[vectors:]

    @pl.when(last)
    def _():
        for q in range(points):
            xout[q] = u[q, 0]
            backward[q].start()
        for b in range(blocks):
            total = filtered_part(0, u[0, b])
            for q in range(1, points):
                total = total + filtered_part(q, u[q, b])
            pf[b] = total

    @pl.when(jnp.logical_not(last))
    def _():
        for q in range(points):
            backward[q].wait_recv()
            xout[q] = u[q, 0] + apply_map(xin[q], Rh[q, 0], Rl[q, 0])[0]

            @pl.when(jnp.logical_not(first))
            def _():
                backward[q].start()

        for b in range(blocks):
            total = None
            for q in range(points):
                if b == 0:
                    x = xout[q]
                else:
                    x = u[q, b] + apply_map(xin[q], Rh[q, b], Rl[q, b])[0]
                part = filtered_part(q, x)
                total = part if total is None else total + part
            pf[b] = total

    share = remote(pf, pfin, one_send.at[0], one_recv.at[0], sib)
    share.start()
    share.wait_recv()
    ff[...] = pf[...] + pfin[...]

    to_left = remote(fsend, fnext, one_send.at[1], one_recv.at[1], left)
    to_right = remote(down, downin, one_send.at[2], one_recv.at[2], right)
    gives_left = jnp.logical_and(core == 0, jnp.logical_not(first))
    gives_right = jnp.logical_and(core == 1, jnp.logical_not(last))

    @pl.when(gives_left)
    def _():
        fsend[...] = ff[0]
        to_left.start()

    @pl.when(gives_right)
    def _():
        down[...] = product(split(ff[blocks - 1]), (Eh[blocks - 1], El[blocks - 1]), NN)
        to_right.start()
        to_left.wait_recv()

    @pl.when(jnp.logical_not(gives_right))
    def _():
        fnext[...] = jnp.zeros_like(fnext)

    gram_plain = jnp.zeros((vectors, vectors), f32)
    gram_matrix = jnp.zeros((vectors, vectors), f32)
    for j in range(mine):
        at = core * mine + j
        block = ff[at]
        filt_ref[:, j * width : (j + 1) * width] = block
        if j < mine - 1:
            upper = ff[at + 1]
        else:
            upper = jnp.where(core == 0, ff[mine], fnext[...])
        halves = split(block)
        up = product(split(upper), (Eh[at], El[at]), NT)
        up_halves = split(up)
        partial = product(halves, split(D[j]), NT) + up
        gram_plain += product(halves, halves, NT)
        gram_matrix += product(halves, split(partial), NT) + product(up_halves, halves, NT)
        app_ref[:, j * width : (j + 1) * width] = partial

    pair = remote(gown, gsib, one_send.at[4], one_recv.at[4], sib)
    gown[0] = gram_plain
    gown[1] = gram_matrix
    pass_on = remote(gown, gin, one_send.at[3], one_recv.at[3], before)

    @pl.when(jnp.logical_not(last))
    def _():
        pass_on.wait_recv()
        gown[...] = gown[...] + gin[...]

    @pl.when(jnp.logical_not(first))
    def _():
        pass_on.start()

    @pl.when(first)
    def _():
        pair.start()
        pair.wait_recv()
        scale = 1.0 / (blocks * width * n)
        gfin[...] = (gown[...] + gsib[...]) * scale

        @pl.loop(1, n)
        def _(other):
            remote(gfin, gfin, all_send.at[other], all_recv, other * 2 + core).start()

    for j in range(mine):
        at = core * mine + j
        if j == 0:
            @pl.when(core == 1)
            def _():
                below = product(split(ff[mine - 1]), (Eh[mine - 1], El[mine - 1]), NN)
                app_ref[:, :width] += below

            @pl.when(gives_left)
            def _():
                to_right.wait_recv()
                app_ref[:, :width] += downin[...]
        else:
            below = product(split(ff[at - 1]), (Eh[at - 1], El[at - 1]), NN)
            app_ref[:, j * width : (j + 1) * width] += below

    @pl.when(jnp.logical_not(first))
    def _():
        remote(gfin, gfin, all_send.at[0], all_recv, core).wait_recv()

    gram_ref[...] = gfin[...]

    share.wait_send()

    @pl.when(gives_left)
    def _():
        to_left.wait_send()

    @pl.when(gives_right)
    def _():
        to_right.wait_send()

    @pl.when(jnp.logical_not(last))
    def _():
        for q in range(points):
            forward[q].wait_send()

    @pl.when(jnp.logical_not(first))
    def _():
        for q in range(points):
            backward[q].wait_send()
        pass_on.wait_send()

    @pl.when(first)
    def _():
        pair.wait_send()

        @pl.loop(1, n)
        def _(other):
            remote(gfin, gfin, all_send.at[other], all_recv, other * 2 + core).wait_send()


def shards(n, subspace, s_inv, couple, diag_blocks, weights):
    points, mine = s_inv.shape[0] // 2, s_inv.shape[1]
    width, vectors = couple.shape[1], subspace.shape[0]
    blocks = 2 * mine
    pivots = s_inv.reshape(2 * points, mine, 2 * width, width)
    square = (blocks, width, width)
    maps = (points, blocks, 2 * width, width)
    state = (points, 2 * vectors, width)
    states = (points, blocks, 2 * vectors, width)
    piece = (vectors, width)
    grams = (2, vectors, vectors)
    scratch = (
        [pltpu.VMEM((2, vectors, mine * width), f32), pltpu.VMEM(maps, f32)]
        + [pltpu.VMEM(square, f32), pltpu.VMEM((mine, width, width), f32)]
        + [pltpu.VMEM(square, bf16)] * 4
        + [pltpu.VMEM((points, blocks, 4 * width, width), bf16)] * 2
        + [pltpu.VMEM(maps, bf16)] * 2
        + [pltpu.VMEM((points, 2 * width, width), bf16)] * 2
        + [pltpu.VMEM(maps, bf16)] * 2
        + [pltpu.VMEM(state, f32)] * 3
        + [pltpu.VMEM(states, f32)] * 2
        + [pltpu.VMEM(state, f32)] * 2
        + [pltpu.VMEM((blocks,) + piece, f32)] * 3
        + [pltpu.VMEM(piece, f32)] * 4
        + [pltpu.VMEM(grams, f32)] * 4
        + [pltpu.SemaphoreType.DMA((4,))]
        + [pltpu.SemaphoreType.DMA((3,))] * 2
        + [pltpu.SemaphoreType.DMA((points,))] * 4
        + [pltpu.SemaphoreType.DMA((5,))] * 2
        + [pltpu.SemaphoreType.DMA((n,)), pltpu.SemaphoreType.DMA]
    )
    whole = pl.BlockSpec(memory_space=pltpu.VMEM)
    anywhere = pl.BlockSpec(memory_space=pl.ANY)
    return pl.pallas_call(
        functools.partial(kernel, n),
        out_shape=(
            jax.ShapeDtypeStruct(subspace.shape, f32),
            jax.ShapeDtypeStruct(subspace.shape, f32),
            jax.ShapeDtypeStruct(grams, f32),
        ),
        in_specs=[anywhere] * 4 + [pl.BlockSpec(memory_space=pltpu.SMEM)],
        out_specs=(whole, whole, whole),
        scratch_shapes=scratch,
        compiler_params=pltpu.CompilerParams(
            collective_id=0, has_side_effects=True, vmem_limit_bytes=48 * 2**20
        ),
        name="filter_pass",
    )(subspace, pivots, couple, diag_blocks, weights)


def solution(mesh):
    placed = (
        P("parts", "chain"),
        P("parts", "chain", None, None, None),
        P("chain", "parts", None),
        P("chain", "parts", None),
        P("parts", None),
    )
    return jax.shard_map(
        functools.partial(shards, mesh.shape["chain"] // 2),
        mesh=mesh,
        in_specs=placed,
        out_specs=(P("parts", "chain"), P("parts", "chain"), P(None, "parts", None)),
        check_vma=False,
    )
```

time: 601 us -> 93.7 us (0.16); the launches traced: 592 us -> 93.4 us
  matrix products: 161 us -> 0 us
  waiting for transfers between devices: 134 us -> 0 us
  starting transfers between devices: 127 us -> 0 us
  Pallas kernels: 0 us -> 85 us
  blocking collectives: 64.7 us -> 0 us
  other arithmetic: 39.4 us -> 0 us
  local copies, waits for them, and re-layouts: 39.9 us -> 7.75 us
  loops' own time: 24.9 us -> 0 us
    dot_general x186 -> x0, matrix products: 161 us -> none  [the longest x30 21.1 us: right_apply(): jnp.einsum('qnk,qkj->qnj', vecs[:, 1], matrix[:, 0], precision=highest)]
    ppermute x32 -> x0, waiting for transfers between devices: 134 us -> none  [passed_along(): return lax.ppermute(shard, axis, pairs)]
    ppermute x32 -> x0, starting transfers between devices: 127 us -> none  [passed_along(): return lax.ppermute(shard, axis, pairs)]
    pallas_call x0 -> x1, Pallas kernels: none -> 85 us  [shards(): pl.pallas_call(functools.partial(kernel, n), out_shape=(jax.ShapeDtypeStr...]
    psum x1 -> x0, blocking collectives: 64.7 us -> none  [shards(): summed = lax.psum(jnp.stack([gram_plain, gram_matrix]), 'chain')]
    add x36 -> x0, other arithmetic: 38.3 us -> none  [the longest x15 25.5 us: backward_hop(): right_apply(inbound, backward_map) + backward_tip]
    another operation x8 -> x0, loops' own time: 24.9 us -> none  [the longest x3 11.8 us: sweep_forward(): return lax.scan(advance, start_rows, jnp.arange(blocks_dev))]
    squeeze x13 -> x0, local copies, waits for them, and re-layouts: 20.8 us -> none  [the longest x6 10.4 us: retreat(): pivot_inv = lax.dynamic_index_in_dim(pivots, position, 1, keepdims=False)]
  transfers between devices with their start and end apart: 32 -> 0, of which waited for: 30 -> 0; matrix products, arithmetic and copies ran while one was open for 0% -> 0% of each run, Pallas kernels for 0% -> 0%
where the time goes in v1:
time: 93.7 us; the launch traced here: 93.4 us
  Pallas kernels  85 us (91%)
  local copies, waits for them, and re-layouts  7.75 us (8%)
    pallas_call x1, Pallas kernels, shards(): pl.pallas_call(functools.partial(kernel, n), out_shape=(jax.ShapeDtypeStr...  85 us
    unnamed x12, local copies, waits for them, and re-layouts  7.75 us

profile of v1, /device:TPU:0, one launch (start us, length us, event | category | flops | bytes accessed | tf_op | source)
XLA Modules:
  0.0 93.4 jit_solution(17404188535711268154)
XLA Ops:
  0.6 0.8 copy.8.w_ref
  1.4 0.0 copy-start
  1.4 2.2 %copy-done = f32[4,2,2,256,256]{4,3,2,1,0:T(8,128)S(1)} copy-done((f32[4,2,2,256,256]{4,3,2,1,0:T(8,128)S(1)}, f32[4,2,2,256,256]{4,3,2,1,0:T(8,128)}, u32[]{:S(2)}) %copy-start) | copy-done | bytes 4194328
  3.6 0.0 copy-start.1
  3.6 1.0 %copy-done.1 = f32[2,256,256]{2,1,0:T(8,128)S(1)} copy-done((f32[2,256,256]{2,1,0:T(8,128)S(1)}, f32[2,256,256]{2,1,0:T(8,128)}, u32[]{:S(2)}) %copy-start.1) | copy-done | bytes 524312
  4.6 0.0 copy-start.2
  4.6 1.0 %copy-done.2 = f32[2,256,256]{2,1,0:T(8,128)S(1)} copy-done((f32[2,256,256]{2,1,0:T(8,128)S(1)}, f32[2,256,256]{2,1,0:T(8,128)}, u32[]{:S(2)}) %copy-start.2) | copy-done | bytes 524312
  5.7 0.0 copy-start.3
  5.7 0.8 copy-done.3
  6.5 85.0 %filter_pass.1 = (f32[32,512]{1,0:T(8,128)S(1)}, f32[32,512]{1,0:T(8,128)S(1)}, f32[2,32,32]{2,1,0:T(8,128)S(1)}) custom-call(f32[32,512]{1,0:T(8,128)S(1)} %copy-done.3, f32[4,2,512,256]{3,2,1,0:T(8,128)S(1)} %bitcast.1, f32[2,256,256]{2,1,0:T(8,128)S(1)} %copy-done.1, f32[2,256,256]{2,1,0:T(8,128)S(1)} %copy-done.2, f32[4,2]{1,0:T(4,128)S(1)} %copy.8.w_ref), custom_call_target="tpu_custom_call" | custom-call | tf_op jit(solution)/shard_map/filter_pass/pallas_call | solution.py:436
  91.5 0.6 copy.12
  92.1 0.6 copy.13
  92.8 0.6 copy.14
Async XLA Ops:
  1.4 2.2 %copy-start = (f32[4,2,2,256,256]{4,3,2,1,0:T(8,128)S(1)}, f32[4,2,2,256,256]{4,3,2,1,0:T(8,128)}, u32[]{:S(2)}) copy-start(f32[4,2,2,256,256]{4,3,2,1,0:T(8,128)} %param.6) | copy-start | bytes 12582916
  3.6 1.0 %copy-start.1 = (f32[2,256,256]{2,1,0:T(8,128)S(1)}, f32[2,256,256]{2,1,0:T(8,128)}, u32[]{:S(2)}) copy-start(f32[2,256,256]{2,1,0:T(8,128)} %e_hbm.1) | copy-start | bytes 1572868
  4.6 1.0 %copy-start.2 = (f32[2,256,256]{2,1,0:T(8,128)S(1)}, f32[2,256,256]{2,1,0:T(8,128)}, u32[]{:S(2)}) copy-start(f32[2,256,256]{2,1,0:T(8,128)} %d_hbm.1) | copy-start | bytes 1572868
  5.7 0.8 copy-start.3

commit v2 on v1

--- a/solution.py
+++ b/solution.py
@@ -16,6 +16,9 @@
 def split(a):
     high = a.astype(bf16)
     return high, (a - high.astype(f32)).astype(bf16)
+
+
+PIECES = 2
 
 
 def dot(a, b, dims):
@@ -40,6 +43,19 @@
     return results
 
 
+def joined(parts):
+    half = parts[0].shape[0] // 2
+    return jnp.concatenate([part[:half] for part in parts] + [part[half:] for part in parts], axis=0)
+
+
+def piece_of(rows, p):
+    half = rows.shape[0] // 2
+    size = half // PIECES
+    return jnp.concatenate(
+        [rows[p * size : (p + 1) * size], rows[half + p * size : half + (p + 1) * size]], axis=0
+    )
+
+
 def compose(a, b):
     width = b[0].shape[1]
     by_re = product(a, (b[0][:width], b[1][:width]), NN)
@@ -48,8 +64,8 @@
 
 
 def kernel(
-    n, f_hbm, s_hbm, e_hbm, d_hbm, w_ref, filt_ref, app_ref, gram_ref,
-    F, S, E, D, Eh, El, Th, Tl, Wh, Wl, Nh, Nl, Ch, Cl, Rh, Rl,
+    n, f_hbm, s_hbm, e_hbm, d_hbm, w_hbm, filt_ref, app_ref, gram_ref,
+    F, S, E, D, w_ref, Eh, El, Th, Tl, Wh, Wl, Nh, Nl, Ch, Cl, Rh, Rl,
     tip, cin, cout, y, u, xin, xout, pf, pfin, ff, fnext, fsend, down, downin,
     gown, gin, gsib, gfin, local_sem, swap_send, swap_recv, fwd_send, fwd_recv,
     bwd_send, bwd_recv, one_send, one_recv, all_send, all_recv,
@@ -84,6 +100,7 @@
         pltpu.make_async_copy(e_hbm, E.at[here], local_sem.at[1]),
         pltpu.make_async_copy(s_hbm.at[own_points], S.at[:, here], local_sem.at[2]),
         pltpu.make_async_copy(d_hbm, D, local_sem.at[3]),
+        pltpu.make_async_copy(w_hbm, w_ref, local_sem.at[4]),
     ]
     for copy in local:
         copy.start()
@@ -124,26 +141,32 @@
         copy.start()
     for copy in local:
         copy.wait()
-    for copy in swap:
-        copy.wait()
-
-    @pl.loop(0, blocks)
-    def _(b):
-        Eh[b], El[b] = split(E[b])
-        Th[b], Tl[b] = split(E[b].T)
-
-    @pl.loop(0, points)
-    def _(q):
-        @pl.loop(0, blocks)
-        def _(b):
-            high, low = split(S[q, b])
-            Wh[q, b, : 2 * width], Wl[q, b, : 2 * width] = high, low
-            turned = (Th[b], Tl[b])
-            for part in range(2):
-                rows = slice(part * width, (part + 1) * width)
-                out = split(product(turned, (high[rows], low[rows]), NN))
-                to = slice((2 + part) * width, (3 + part) * width)
-                Wh[q, b, to], Wl[q, b, to] = out
+
+    @pl.loop(0, 2)
+    def _(turn):
+        @pl.when(turn == 1)
+        def _():
+            for copy in swap:
+                copy.wait()
+
+        start = lax.rem(core + turn, 2) * mine
+
+        @pl.loop(0, mine)
+        def _(j):
+            b = start + j
+            Eh[b], El[b] = split(E[b])
+            turned = split(E[b].T)
+            Th[b], Tl[b] = turned
+
+            @pl.loop(0, points)
+            def _(q):
+                high, low = split(S[q, b])
+                Wh[q, b, : 2 * width], Wl[q, b, : 2 * width] = high, low
+                for part in range(2):
+                    rows = slice(part * width, (part + 1) * width)
+                    out = split(product(turned, (high[rows], low[rows]), NN))
+                    to = slice((2 + part) * width, (3 + part) * width)
+                    Wh[q, b, to], Wl[q, b, to] = out
 
     def source(b):
         rows = F[b // mine, :, (b % mine) * width : (b % mine + 1) * width]
@@ -156,7 +179,8 @@
             z = source(b) if b == 0 else source(b) + carried[q]
             (carried[q],) = apply_map(z, Wh[q, b, low_rows], Wl[q, b, low_rows])
     for q in range(points):
-        tip[q] = carried[q]
+        for p in range(PIECES):
+            tip[q, p] = piece_of(carried[q], p)
 
     @pl.when(jnp.logical_and(jnp.logical_not(first), jnp.logical_not(last)))
     def _():
@@ -170,33 +194,33 @@
                     compose((Wh[q, b, low_rows], Wl[q, b, low_rows]), (Ch[q], Cl[q]))
                 )
 
+    parts = [(q, p) for q in range(points) for p in range(PIECES)]
     forward = [
-        remote(cout.at[q], cin.at[q], fwd_send.at[q], fwd_recv.at[q], after) for q in range(points)
+        remote(cout.at[at], cin.at[at], fwd_send.at[at], fwd_recv.at[at], after) for at in parts
     ]
     backward = [
-        remote(xout.at[q], xin.at[q], bwd_send.at[q], bwd_recv.at[q], before)
-        for q in range(points)
+        remote(xout.at[at], xin.at[at], bwd_send.at[at], bwd_recv.at[at], before) for at in parts
     ]
 
     def sweep_forward():
         @pl.when(first)
         def _():
-            for q in range(points):
-                cout[q] = tip[q]
-                forward[q].start()
+            for at, copy in zip(parts, forward):
+                cout[at] = tip[at]
+                copy.start()
             cin[...] = jnp.zeros_like(cin)
 
         @pl.when(jnp.logical_not(first))
         def _():
-            for q in range(points):
-                forward[q].wait_recv()
+            for at, copy in zip(parts, forward):
+                copy.wait_recv()
 
                 @pl.when(jnp.logical_not(last))
                 def _():
-                    cout[q] = tip[q] + apply_map(cin[q], Ch[q], Cl[q])[0]
-                    forward[q].start()
-
-        entering = [cin[q] for q in range(points)]
+                    cout[at] = tip[at] + apply_map(cin[at], Ch[at[0]], Cl[at[0]])[0]
+                    copy.start()
+
+        entering = [joined([cin[q, p] for p in range(PIECES)]) for q in range(points)]
         for b in range(blocks):
             for q in range(points):
                 z = source(b) + entering[q]
@@ -242,17 +266,18 @@
                 carried[q] = y[q, b] + apply_map(carried[q], Nh[q, b], Nl[q, b])[0]
             u[q, b] = carried[q]
 
-    weight_re = [w_ref[core * points + q, 0] for q in range(points)]
-    weight_im = [w_ref[core * points + q, 1] for q in range(points)]
+    own_weights = jnp.where(core == 0, w_ref[:, :points], w_ref[:, points:])
+    weight_re = [own_weights[0:1, q : q + 1] for q in range(points)]
+    weight_im = [own_weights[1:2, q : q + 1] for q in range(points)]
 
     def filtered_part(q, x):
         return weight_re[q] * x[:vectors] - weight_im[q] * x[vectors:]
 
     @pl.when(last)
     def _():
-        for q in range(points):
-            xout[q] = u[q, 0]
-            backward[q].start()
+        for at, copy in zip(parts, backward):
+            xout[at] = piece_of(u[at[0], 0], at[1])
+            copy.start()
         for b in range(blocks):
             total = filtered_part(0, u[0, b])
             for q in range(1, points):
@@ -261,24 +286,25 @@
 
     @pl.when(jnp.logical_not(last))
     def _():
-        for q in range(points):
-            backward[q].wait_recv()
-            xout[q] = u[q, 0] + apply_map(xin[q], Rh[q, 0], Rl[q, 0])[0]
+        for at, copy in zip(parts, backward):
+            copy.wait_recv()
 
             @pl.when(jnp.logical_not(first))
             def _():
-                backward[q].start()
-
+                known = piece_of(u[at[0], 0], at[1])
+                xout[at] = known + apply_map(xin[at], Rh[at[0], 0], Rl[at[0], 0])[0]
+                copy.start()
+
+        totals = [None] * blocks
+        for q in range(points):
+            entering = joined([xin[q, p] for p in range(PIECES)])
+            flat = (blocks * 2 * width, width)
+            moved = apply_map(entering, Rh[q].reshape(flat), Rl[q].reshape(flat))
+            for b in range(blocks):
+                part = filtered_part(q, u[q, b] + moved[b])
+                totals[b] = part if q == 0 else totals[b] + part
         for b in range(blocks):
-            total = None
-            for q in range(points):
-                if b == 0:
-                    x = xout[q]
-                else:
-                    x = u[q, b] + apply_map(xin[q], Rh[q, b], Rl[q, b])[0]
-                part = filtered_part(q, x)
-                total = part if total is None else total + part
-            pf[b] = total
+            pf[b] = totals[b]
 
     share = remote(pf, pfin, one_send.at[0], one_recv.at[0], sib)
     share.start()
@@ -305,8 +331,7 @@
     def _():
         fnext[...] = jnp.zeros_like(fnext)
 
-    gram_plain = jnp.zeros((vectors, vectors), f32)
-    gram_matrix = jnp.zeros((vectors, vectors), f32)
+    grams = jnp.zeros((vectors, 4 * vectors), f32)
     for j in range(mine):
         at = core * mine + j
         block = ff[at]
@@ -319,13 +344,15 @@
         up = product(split(upper), (Eh[at], El[at]), NT)
         up_halves = split(up)
         partial = product(halves, split(D[j]), NT) + up
-        gram_plain += product(halves, halves, NT)
-        gram_matrix += product(halves, split(partial), NT) + product(up_halves, halves, NT)
+        blank = jnp.zeros_like(block)
+        grams += product(halves, split(jnp.concatenate([block, partial, blank, blank], axis=0)), NT)
+        grams += product(
+            up_halves, split(jnp.concatenate([blank, block, blank, blank], axis=0)), NT
+        )
         app_ref[:, j * width : (j + 1) * width] = partial
 
     pair = remote(gown, gsib, one_send.at[4], one_recv.at[4], sib)
-    gown[0] = gram_plain
-    gown[1] = gram_matrix
+    gown[...] = grams
     pass_on = remote(gown, gin, one_send.at[3], one_recv.at[3], before)
 
     @pl.when(jnp.logical_not(last))
@@ -368,7 +395,8 @@
     def _():
         remote(gfin, gfin, all_send.at[0], all_recv, core).wait_recv()
 
-    gram_ref[...] = gfin[...]
+    gram_ref[0] = gfin[:, :vectors]
+    gram_ref[1] = gfin[:, vectors : 2 * vectors]
 
     share.wait_send()
 
@@ -382,13 +410,13 @@
 
     @pl.when(jnp.logical_not(last))
     def _():
-        for q in range(points):
-            forward[q].wait_send()
+        for copy in forward:
+            copy.wait_send()
 
     @pl.when(jnp.logical_not(first))
     def _():
-        for q in range(points):
-            backward[q].wait_send()
+        for copy in backward:
+            copy.wait_send()
         pass_on.wait_send()
 
     @pl.when(first)
@@ -407,13 +435,14 @@
     pivots = s_inv.reshape(2 * points, mine, 2 * width, width)
     square = (blocks, width, width)
     maps = (points, blocks, 2 * width, width)
-    state = (points, 2 * vectors, width)
+    state = (points, PIECES, 2 * vectors // PIECES, width)
     states = (points, blocks, 2 * vectors, width)
     piece = (vectors, width)
     grams = (2, vectors, vectors)
     scratch = (
         [pltpu.VMEM((2, vectors, mine * width), f32), pltpu.VMEM(maps, f32)]
         + [pltpu.VMEM(square, f32), pltpu.VMEM((mine, width, width), f32)]
+        + [pltpu.VMEM((2, 2 * points), f32)]
         + [pltpu.VMEM(square, bf16)] * 4
         + [pltpu.VMEM((points, blocks, 4 * width, width), bf16)] * 2
         + [pltpu.VMEM(maps, bf16)] * 2
@@ -424,10 +453,10 @@
         + [pltpu.VMEM(state, f32)] * 2
         + [pltpu.VMEM((blocks,) + piece, f32)] * 3
         + [pltpu.VMEM(piece, f32)] * 4
-        + [pltpu.VMEM(grams, f32)] * 4
-        + [pltpu.SemaphoreType.DMA((4,))]
+        + [pltpu.VMEM((vectors, 4 * vectors), f32)] * 4
+        + [pltpu.SemaphoreType.DMA((5,))]
         + [pltpu.SemaphoreType.DMA((3,))] * 2
-        + [pltpu.SemaphoreType.DMA((points,))] * 4
+        + [pltpu.SemaphoreType.DMA((points, PIECES))] * 4
         + [pltpu.SemaphoreType.DMA((5,))] * 2
         + [pltpu.SemaphoreType.DMA((n,)), pltpu.SemaphoreType.DMA]
     )
@@ -440,14 +469,14 @@
             jax.ShapeDtypeStruct(subspace.shape, f32),
             jax.ShapeDtypeStruct(grams, f32),
         ),
-        in_specs=[anywhere] * 4 + [pl.BlockSpec(memory_space=pltpu.SMEM)],
+        in_specs=[anywhere] * 5,
         out_specs=(whole, whole, whole),
         scratch_shapes=scratch,
         compiler_params=pltpu.CompilerParams(
-            collective_id=0, has_side_effects=True, vmem_limit_bytes=48 * 2**20
+            collective_id=0, has_side_effects=True, vmem_limit_bytes=63 * 2**20
         ),
         name="filter_pass",
-    )(subspace, pivots, couple, diag_blocks, weights)
+    )(subspace, pivots, couple, diag_blocks, weights.T)
 
 
 def solution(mesh):

time: 93.7 us -> 81 us (0.86)
  Pallas kernels: 85 us -> 75.8 us
  local copies, waits for them, and re-layouts: 7.75 us -> 4.32 us
    pallas_call x1, Pallas kernels: 85 us -> 75.8 us  [shards(): pl.pallas_call(functools.partial(kernel, n), out_shape=(jax.ShapeDtypeStr...]
    unnamed x12 -> x3, local copies, waits for them, and re-layouts: 7.75 us -> 4.32 us
where the time goes in v2:
time: 81 us; the launch traced here: 80.7 us
  Pallas kernels  75.8 us (94%)
  local copies, waits for them, and re-layouts  4.32 us (5%)
    pallas_call x1, Pallas kernels, shards(): pl.pallas_call(functools.partial(kernel, n), out_shape=(jax.ShapeDtypeStr...  75.8 us
    unnamed x3, local copies, waits for them, and re-layouts  4.32 us

profile of v2, /device:TPU:0, one launch (start us, length us, event | category | flops | bytes accessed | tf_op | source)
XLA Modules:
  0.0 80.7 jit_solution(13069397593453124520)
XLA Ops:
  0.6 75.8 %filter_pass.1 = (f32[32,512]{1,0:T(8,128)}, f32[32,512]{1,0:T(8,128)}, f32[2,32,32]{2,1,0:T(8,128)}) custom-call(f32[32,512]{1,0:T(8,128)} %f_hbm.1, f32[4,2,512,256]{3,2,1,0:T(8,128)} %bitcast.2, f32[2,256,256]{2,1,0:T(8,128)} %e_hbm.1, f32[2,256,256]{2,1,0:T(8,128)} %d_hbm.1, f32[2,4]{1,0:T(2,128)} %bitcast.3), custom_call_target="tpu_custom_call" | custom-call | tf_op jit(solution)/shard_map/filter_pass/pallas_call | solution.py:465
  76.4 1.5 %copy.11 = f32[32,512]{1,0:T(8,128)} copy(f32[32,512]{1,0:T(8,128)} %get-tuple-element.6) | data formatting | bytes 131072
  77.9 1.5 %copy.12 = f32[32,512]{1,0:T(8,128)} copy(f32[32,512]{1,0:T(8,128)} %get-tuple-element.7) | data formatting | bytes 131072
  79.3 1.4 %copy.13 = f32[2,32,32]{2,1,0:T(8,128)} copy(f32[2,32,32]{2,1,0:T(8,128)} %get-tuple-element.8) | data formatting | bytes 16384

commit v3 on v2

--- a/solution.py
+++ b/solution.py
@@ -18,7 +18,7 @@
     return high, (a - high.astype(f32)).astype(bf16)
 
 
-PIECES = 2
+PIECES = 4
 
 
 def dot(a, b, dims):
@@ -41,6 +41,13 @@
             jnp.concatenate([by_re[:half] - by_im[half:], by_re[half:] + by_im[:half]], axis=0)
         )
     return results
+
+
+def apply_real(rows, high, low):
+    count = rows.shape[0]
+    rows_high, rows_low = split(rows)
+    both = dot(jnp.concatenate([rows_high, rows_low], axis=0), high, NN)
+    return both[:count] + (both[count:] + dot(rows_high, low, NN))
 
 
 def joined(parts):
@@ -78,6 +85,8 @@
     right = jnp.minimum(me + 1, 2 * n - 1)
     left = jnp.maximum(me - 1, 0)
     first, last = chip == 0, chip == n - 1
+    near = chip < 2
+    far = jnp.logical_not(near)
     points, blocks = S.shape[0], S.shape[1]
     mine = e_hbm.shape[0]
     width = e_hbm.shape[1]
@@ -162,27 +171,33 @@
             def _(q):
                 high, low = split(S[q, b])
                 Wh[q, b, : 2 * width], Wl[q, b, : 2 * width] = high, low
-                for part in range(2):
-                    rows = slice(part * width, (part + 1) * width)
-                    out = split(product(turned, (high[rows], low[rows]), NN))
-                    to = slice((2 + part) * width, (3 + part) * width)
-                    Wh[q, b, to], Wl[q, b, to] = out
+
+                @pl.when(far)
+                def _():
+                    for part in range(2):
+                        rows = slice(part * width, (part + 1) * width)
+                        out = split(product(turned, (high[rows], low[rows]), NN))
+                        to = slice((2 + part) * width, (3 + part) * width)
+                        Wh[q, b, to], Wl[q, b, to] = out
 
     def source(b):
         rows = F[b // mine, :, (b % mine) * width : (b % mine + 1) * width]
         return jnp.concatenate([rows, jnp.zeros_like(rows)], axis=0)
 
     low_rows = slice(2 * width, 4 * width)
-    carried = [None] * points
-    for b in range(blocks):
+
+    @pl.when(far)
+    def _():
+        carried = [None] * points
+        for b in range(blocks):
+            for q in range(points):
+                z = source(b) if b == 0 else source(b) + carried[q]
+                (carried[q],) = apply_map(z, Wh[q, b, low_rows], Wl[q, b, low_rows])
         for q in range(points):
-            z = source(b) if b == 0 else source(b) + carried[q]
-            (carried[q],) = apply_map(z, Wh[q, b, low_rows], Wl[q, b, low_rows])
-    for q in range(points):
-        for p in range(PIECES):
-            tip[q, p] = piece_of(carried[q], p)
-
-    @pl.when(jnp.logical_and(jnp.logical_not(first), jnp.logical_not(last)))
+            for p in range(PIECES):
+                tip[q, p] = piece_of(carried[q], p)
+
+    @pl.when(jnp.logical_and(far, jnp.logical_not(last)))
     def _():
         @pl.loop(0, points)
         def _(q):
@@ -202,25 +217,44 @@
         remote(xout.at[at], xin.at[at], bwd_send.at[at], bwd_recv.at[at], before) for at in parts
     ]
 
-    def sweep_forward():
+    def entering_rows():
+        return [joined([cin[q, p] for p in range(PIECES)]) for q in range(points)]
+
+    def sweep_near():
         @pl.when(first)
         def _():
+            cin[...] = jnp.zeros_like(cin)
+
+        @pl.when(jnp.logical_not(first))
+        def _():
+            for copy in forward:
+                copy.wait_recv()
+
+        entering = entering_rows()
+        for b in range(blocks):
+            for q in range(points):
+                solved = apply_map(
+                    source(b) + entering[q], Wh[q, b, : 2 * width], Wl[q, b, : 2 * width]
+                )[0]
+                y[q, b] = solved
+                entering[q] = apply_real(solved, Eh[b], El[b])
+
+        @pl.when(jnp.logical_not(last))
+        def _():
             for at, copy in zip(parts, forward):
-                cout[at] = tip[at]
+                cout[at] = piece_of(entering[at[0]], at[1])
                 copy.start()
-            cin[...] = jnp.zeros_like(cin)
-
-        @pl.when(jnp.logical_not(first))
-        def _():
-            for at, copy in zip(parts, forward):
-                copy.wait_recv()
-
-                @pl.when(jnp.logical_not(last))
-                def _():
-                    cout[at] = tip[at] + apply_map(cin[at], Ch[at[0]], Cl[at[0]])[0]
-                    copy.start()
-
-        entering = [joined([cin[q, p] for p in range(PIECES)]) for q in range(points)]
+
+    def sweep_far():
+        for at, copy in zip(parts, forward):
+            copy.wait_recv()
+
+            @pl.when(jnp.logical_not(last))
+            def _():
+                cout[at] = tip[at] + apply_map(cin[at], Ch[at[0]], Cl[at[0]])[0]
+                copy.start()
+
+        entering = entering_rows()
         for b in range(blocks):
             for q in range(points):
                 z = source(b) + entering[q]
@@ -245,13 +279,17 @@
                         compose((Nh[q, b], Nl[q, b]), (Rh[q, b + 1], Rl[q, b + 1]))
                     )
 
-    maps_first = chip * 2 >= n
+    maps_first = chip >= n - 2
 
     @pl.loop(0, 3)
     def _(step):
-        @pl.when(step == 1)
-        def _():
-            sweep_forward()
+        @pl.when(jnp.logical_and(step == 1, near))
+        def _():
+            sweep_near()
+
+        @pl.when(jnp.logical_and(step == 1, far))
+        def _():
+            sweep_far()
 
         @pl.when(step == jnp.where(maps_first, 0, 2))
         def _():
@@ -426,6 +464,31 @@
         @pl.loop(1, n)
         def _(other):
             remote(gfin, gfin, all_send.at[other], all_recv, other * 2 + core).wait_send()
+
+
+def handing(*refs):
+    sources, targets, sems = refs[:3], refs[3:6], refs[6]
+    copies = [
+        pltpu.make_async_copy(source, target, sems.at[i])
+        for i, (source, target) in enumerate(zip(sources, targets))
+    ]
+    for copy in copies:
+        copy.start()
+    for copy in copies:
+        copy.wait()
+
+
+def hand_out(outputs):
+    anywhere = pl.BlockSpec(memory_space=pl.ANY)
+    return pl.pallas_call(
+        handing,
+        out_shape=tuple(jax.ShapeDtypeStruct(out.shape, out.dtype) for out in outputs),
+        in_specs=[anywhere] * 3,
+        out_specs=(anywhere,) * 3,
+        scratch_shapes=[pltpu.SemaphoreType.DMA((3,))],
+        compiler_params=pltpu.CompilerParams(vmem_limit_bytes=63 * 2**20),
+        name="hand_out",
+    )(*outputs)
 
 
 def shards(n, subspace, s_inv, couple, diag_blocks, weights):
@@ -462,7 +525,7 @@
     )
     whole = pl.BlockSpec(memory_space=pltpu.VMEM)
     anywhere = pl.BlockSpec(memory_space=pl.ANY)
-    return pl.pallas_call(
+    outputs = pl.pallas_call(
         functools.partial(kernel, n),
         out_shape=(
             jax.ShapeDtypeStruct(subspace.shape, f32),
@@ -477,6 +540,7 @@
         ),
         name="filter_pass",
     )(subspace, pivots, couple, diag_blocks, weights.T)
+    return tuple(hand_out(outputs))
 
 
 def solution(mesh):

time: 81 us -> 87.3 us (1.078)
  Pallas kernels: 75.8 us -> 86.6 us
  local copies, waits for them, and re-layouts: 4.32 us -> 0 us
    pallas_call x0 -> x1, Pallas kernels: none -> 6.09 us  [hand_out(): pl.pallas_call(handing, out_shape=tuple((jax.ShapeDtypeStruct(out.shape,...]
    pallas_call x1, Pallas kernels: 75.8 us -> 80.5 us  [shards(): pl.pallas_call(functools.partial(kernel, n), out_shape=(jax.ShapeDtypeStr...]
    unnamed x3 -> x0, local copies, waits for them, and re-layouts: 4.32 us -> none
where the time goes in v3:
time: 87.3 us; the launch traced here: 87.2 us
  Pallas kernels  86.6 us (99%)
    pallas_call x1, Pallas kernels, shards(): pl.pallas_call(functools.partial(kernel, n), out_shape=(jax.ShapeDtypeStr...  80.5 us
    pallas_call x1, Pallas kernels, hand_out(): pl.pallas_call(handing, out_shape=tuple((jax.ShapeDtypeStruct(out.shape,...  6.09 us

profile of v3, /device:TPU:0, one launch (start us, length us, event | category | flops | bytes accessed | tf_op | source)
XLA Modules:
  0.0 87.2 jit_solution(14135376057697568630)
XLA Ops:
  0.6 80.5 %filter_pass.1 = (f32[32,512]{1,0:T(8,128)}, f32[32,512]{1,0:T(8,128)}, f32[2,32,32]{2,1,0:T(8,128)}) custom-call(f32[32,512]{1,0:T(8,128)} %f_hbm.1, f32[4,2,512,256]{3,2,1,0:T(8,128)} %bitcast.2, f32[2,256,256]{2,1,0:T(8,128)} %e_hbm.1, f32[2,256,256]{2,1,0:T(8,128)} %d_hbm.1, f32[2,4]{1,0:T(2,128)} %bitcast.3), custom_call_target="tpu_custom_call" | custom-call | tf_op jit(solution)/shard_map/filter_pass/pallas_call | solution.py:528
  81.1 6.1 %hand_out.1 = (f32[32,512]{1,0:T(8,128)}, f32[32,512]{1,0:T(8,128)}, f32[2,32,32]{2,1,0:T(8,128)}) custom-call(f32[32,512]{1,0:T(8,128)} %get-tuple-element.6.refs_0_, f32[32,512]{1,0:T(8,128)} %get-tuple-element.7.refs_1_, f32[2,32,32]{2,1,0:T(8,128)} %get-tuple-element.8.refs_2_), custom_call_target="tpu_custom_call" | custom-call | tf_op jit(solution)/shard_map/hand_out/pallas_call | solution.py:483

commit v4 on v3

--- a/solution.py
+++ b/solution.py
@@ -18,7 +18,7 @@
     return high, (a - high.astype(f32)).astype(bf16)
 
 
-PIECES = 4
+PIECES = 2
 
 
 def dot(a, b, dims):
@@ -32,15 +32,16 @@
 def apply_map(rows, high, low):
     half, width = rows.shape[0] // 2, rows.shape[1]
     rows_high, rows_low = split(rows)
-    both = dot(jnp.concatenate([rows_high, rows_low], axis=0), high, NT)
-    mixed = both[: 2 * half] + (both[2 * half :] + dot(rows_high, low, NT))
-    results = []
-    for at in range(0, mixed.shape[1], 2 * width):
-        by_re, by_im = mixed[:, at : at + width], mixed[:, at + width : at + 2 * width]
-        results.append(
-            jnp.concatenate([by_re[:half] - by_im[half:], by_re[half:] + by_im[:half]], axis=0)
-        )
-    return results
+    stacked = jnp.concatenate([rows_high, rows_low], axis=0)
+    mixed = []
+    for at in range(0, high.shape[0], width):
+        both = dot(stacked, high[at : at + width], NN)
+        fine = dot(rows_high, low[at : at + width], NN)
+        mixed.append(both[: 2 * half] + (both[2 * half :] + fine))
+    return [
+        jnp.concatenate([by_re[:half] - by_im[half:], by_re[half:] + by_im[:half]], axis=0)
+        for by_re, by_im in zip(mixed[::2], mixed[1::2])
+    ]
 
 
 def apply_real(rows, high, low):
@@ -85,7 +86,7 @@
     right = jnp.minimum(me + 1, 2 * n - 1)
     left = jnp.maximum(me - 1, 0)
     first, last = chip == 0, chip == n - 1
-    near = chip < 2
+    near = first
     far = jnp.logical_not(near)
     points, blocks = S.shape[0], S.shape[1]
     mine = e_hbm.shape[0]
@@ -164,21 +165,19 @@
         def _(j):
             b = start + j
             Eh[b], El[b] = split(E[b])
-            turned = split(E[b].T)
-            Th[b], Tl[b] = turned
+            Th[b], Tl[b] = split(E[b].T)
 
             @pl.loop(0, points)
             def _(q):
-                high, low = split(S[q, b])
-                Wh[q, b, : 2 * width], Wl[q, b, : 2 * width] = high, low
+                for part in range(2):
+                    to = slice(part * width, (part + 1) * width)
+                    Wh[q, b, to], Wl[q, b, to] = split(S[q, b, to].T)
 
                 @pl.when(far)
                 def _():
-                    for part in range(2):
-                        rows = slice(part * width, (part + 1) * width)
-                        out = split(product(turned, (high[rows], low[rows]), NN))
-                        to = slice((2 + part) * width, (3 + part) * width)
-                        Wh[q, b, to], Wl[q, b, to] = out
+                    pivot = (Wh[q, b, : 2 * width], Wl[q, b, : 2 * width])
+                    out = split(product(pivot, (Eh[b], El[b]), NN))
+                    Wh[q, b, 2 * width :], Wl[q, b, 2 * width :] = out
 
     def source(b):
         rows = F[b // mine, :, (b % mine) * width : (b % mine + 1) * width]
@@ -206,7 +205,7 @@
             @pl.loop(1, blocks)
             def _(b):
                 Ch[q], Cl[q] = split(
-                    compose((Wh[q, b, low_rows], Wl[q, b, low_rows]), (Ch[q], Cl[q]))
+                    compose((Ch[q], Cl[q]), (Wh[q, b, low_rows], Wl[q, b, low_rows]))
                 )
 
     parts = [(q, p) for q in range(points) for p in range(PIECES)]
@@ -265,8 +264,10 @@
         def _(q):
             @pl.loop(0, blocks)
             def _(b):
-                pivot = (Wh[q, b, : 2 * width], Wl[q, b, : 2 * width])
-                Nh[q, b], Nl[q, b] = split(product(pivot, (Eh[b], El[b]), NN))
+                for part in range(2):
+                    to = slice(part * width, (part + 1) * width)
+                    turned = product((Th[b], Tl[b]), (Wh[q, b, to], Wl[q, b, to]), NN)
+                    Nh[q, b, to], Nl[q, b, to] = split(turned)
 
             @pl.when(jnp.logical_not(last))
             def _():
@@ -276,10 +277,10 @@
                 def _(step):
                     b = blocks - 1 - step
                     Rh[q, b], Rl[q, b] = split(
-                        compose((Nh[q, b], Nl[q, b]), (Rh[q, b + 1], Rl[q, b + 1]))
+                        compose((Rh[q, b + 1], Rl[q, b + 1]), (Nh[q, b], Nl[q, b]))
                     )
 
-    maps_first = chip >= n - 2
+    maps_first = chip * 2 >= n
 
     @pl.loop(0, 3)
     def _(step):
@@ -379,7 +380,7 @@
         else:
             upper = jnp.where(core == 0, ff[mine], fnext[...])
         halves = split(block)
-        up = product(split(upper), (Eh[at], El[at]), NT)
+        up = product(split(upper), (Th[at], Tl[at]), NN)
         up_halves = split(up)
         partial = product(halves, split(D[j]), NT) + up
         blank = jnp.zeros_like(block)
@@ -464,31 +465,6 @@
         @pl.loop(1, n)
         def _(other):
             remote(gfin, gfin, all_send.at[other], all_recv, other * 2 + core).wait_send()
-
-
-def handing(*refs):
-    sources, targets, sems = refs[:3], refs[3:6], refs[6]
-    copies = [
-        pltpu.make_async_copy(source, target, sems.at[i])
-        for i, (source, target) in enumerate(zip(sources, targets))
-    ]
-    for copy in copies:
-        copy.start()
-    for copy in copies:
-        copy.wait()
-
-
-def hand_out(outputs):
-    anywhere = pl.BlockSpec(memory_space=pl.ANY)
-    return pl.pallas_call(
-        handing,
-        out_shape=tuple(jax.ShapeDtypeStruct(out.shape, out.dtype) for out in outputs),
-        in_specs=[anywhere] * 3,
-        out_specs=(anywhere,) * 3,
-        scratch_shapes=[pltpu.SemaphoreType.DMA((3,))],
-        compiler_params=pltpu.CompilerParams(vmem_limit_bytes=63 * 2**20),
-        name="hand_out",
-    )(*outputs)
 
 
 def shards(n, subspace, s_inv, couple, diag_blocks, weights):
@@ -525,7 +501,7 @@
     )
     whole = pl.BlockSpec(memory_space=pltpu.VMEM)
     anywhere = pl.BlockSpec(memory_space=pl.ANY)
-    outputs = pl.pallas_call(
+    return pl.pallas_call(
         functools.partial(kernel, n),
         out_shape=(
             jax.ShapeDtypeStruct(subspace.shape, f32),
@@ -540,7 +516,6 @@
         ),
         name="filter_pass",
     )(subspace, pivots, couple, diag_blocks, weights.T)
-    return tuple(hand_out(outputs))
 
 
 def solution(mesh):

time: 87.3 us -> 78.2 us (0.90)
  Pallas kernels: 86.6 us -> 73 us
  local copies, waits for them, and re-layouts: 0 us -> 4.32 us
    pallas_call x1, Pallas kernels: 80.5 us -> 73 us  [shards(): pl.pallas_call(functools.partial(kernel, n), out_shape=(jax.ShapeDtypeStr...]
    pallas_call x1 -> x0, Pallas kernels: 6.09 us -> none  [hand_out(): pl.pallas_call(handing, out_shape=tuple((jax.ShapeDtypeStruct(out.shape,...]
    unnamed x0 -> x3, local copies, waits for them, and re-layouts: none -> 4.32 us
where the time goes in v4:
time: 78.2 us; the launch traced here: 78 us
  Pallas kernels  73 us (93%)
  local copies, waits for them, and re-layouts  4.32 us (6%)
    pallas_call x1, Pallas kernels, shards(): pl.pallas_call(functools.partial(kernel, n), out_shape=(jax.ShapeDtypeStr...  73 us
    unnamed x3, local copies, waits for them, and re-layouts  4.32 us

profile of v4, /device:TPU:0, one launch (start us, length us, event | category | flops | bytes accessed | tf_op | source)
XLA Modules:
  0.0 78.0 jit_solution(7900644770842880321)
XLA Ops:
  0.6 73.0 %filter_pass.1 = (f32[32,512]{1,0:T(8,128)}, f32[32,512]{1,0:T(8,128)}, f32[2,32,32]{2,1,0:T(8,128)}) custom-call(f32[32,512]{1,0:T(8,128)} %f_hbm.1, f32[4,2,512,256]{3,2,1,0:T(8,128)} %bitcast.2, f32[2,256,256]{2,1,0:T(8,128)} %e_hbm.1, f32[2,256,256]{2,1,0:T(8,128)} %d_hbm.1, f32[2,4]{1,0:T(2,128)} %bitcast.3), custom_call_target="tpu_custom_call" | custom-call | tf_op jit(solution)/shard_map/filter_pass/pallas_call | solution.py:504
  73.6 1.5 %copy.11 = f32[32,512]{1,0:T(8,128)} copy(f32[32,512]{1,0:T(8,128)} %get-tuple-element.6) | data formatting | bytes 131072
  75.1 1.5 %copy.12 = f32[32,512]{1,0:T(8,128)} copy(f32[32,512]{1,0:T(8,128)} %get-tuple-element.7) | data formatting | bytes 131072
  76.6 1.4 %copy.13 = f32[2,32,32]{2,1,0:T(8,128)} copy(f32[2,32,32]{2,1,0:T(8,128)} %get-tuple-element.8) | data formatting | bytes 16384

commit v5 on v4

--- a/solution.py
+++ b/solution.py
@@ -88,6 +88,7 @@
     first, last = chip == 0, chip == n - 1
     near = first
     far = jnp.logical_not(near)
+    composed = jnp.logical_and(chip > 1, jnp.logical_not(last))
     points, blocks = S.shape[0], S.shape[1]
     mine = e_hbm.shape[0]
     width = e_hbm.shape[1]
@@ -185,7 +186,7 @@
 
     low_rows = slice(2 * width, 4 * width)
 
-    @pl.when(far)
+    @pl.when(composed)
     def _():
         carried = [None] * points
         for b in range(blocks):
@@ -196,7 +197,7 @@
             for p in range(PIECES):
                 tip[q, p] = piece_of(carried[q], p)
 
-    @pl.when(jnp.logical_and(far, jnp.logical_not(last)))
+    @pl.when(composed)
     def _():
         @pl.loop(0, points)
         def _(q):
@@ -248,7 +249,7 @@
         for at, copy in zip(parts, forward):
             copy.wait_recv()
 
-            @pl.when(jnp.logical_not(last))
+            @pl.when(composed)
             def _():
                 cout[at] = tip[at] + apply_map(cin[at], Ch[at[0]], Cl[at[0]])[0]
                 copy.start()
@@ -258,6 +259,12 @@
             for q in range(points):
                 z = source(b) + entering[q]
                 y[q, b], entering[q] = apply_map(z, Wh[q, b], Wl[q, b])
+
+        @pl.when(jnp.logical_and(chip == 1, jnp.logical_not(last)))
+        def _():
+            for at, copy in zip(parts, forward):
+                cout[at] = piece_of(entering[at[0]], at[1])
+                copy.start()
 
     def backward_maps():
         @pl.loop(0, points)
@@ -280,7 +287,7 @@
                         compose((Rh[q, b + 1], Rl[q, b + 1]), (Nh[q, b], Nl[q, b]))
                     )
 
-    maps_first = chip * 2 >= n
+    maps_first = chip * 8 >= 5 * n
 
     @pl.loop(0, 3)
     def _(step):

time: 78.2 us -> 81.2 us (1.038)
  Pallas kernels: 73 us -> 76 us
    pallas_call x1, Pallas kernels: 73 us -> 76 us  [shards(): pl.pallas_call(functools.partial(kernel, n), out_shape=(jax.ShapeDtypeStr...]
where the time goes in v5:
time: 81.2 us; the launch traced here: 80.9 us
  Pallas kernels  76 us (94%)
  local copies, waits for them, and re-layouts  4.32 us (5%)
    pallas_call x1, Pallas kernels, shards(): pl.pallas_call(functools.partial(kernel, n), out_shape=(jax.ShapeDtypeStr...  76 us
    unnamed x3, local copies, waits for them, and re-layouts  4.32 us

profile of v5, /device:TPU:0, one launch (start us, length us, event | category | flops | bytes accessed | tf_op | source)
XLA Modules:
  0.0 80.9 jit_solution(3702841977407215640)
XLA Ops:
  0.6 76.0 %filter_pass.1 = (f32[32,512]{1,0:T(8,128)}, f32[32,512]{1,0:T(8,128)}, f32[2,32,32]{2,1,0:T(8,128)}) custom-call(f32[32,512]{1,0:T(8,128)} %f_hbm.1, f32[4,2,512,256]{3,2,1,0:T(8,128)} %bitcast.2, f32[2,256,256]{2,1,0:T(8,128)} %e_hbm.1, f32[2,256,256]{2,1,0:T(8,128)} %d_hbm.1, f32[2,4]{1,0:T(2,128)} %bitcast.3), custom_call_target="tpu_custom_call" | custom-call | tf_op jit(solution)/shard_map/filter_pass/pallas_call | solution.py:511
  76.6 1.5 %copy.11 = f32[32,512]{1,0:T(8,128)} copy(f32[32,512]{1,0:T(8,128)} %get-tuple-element.6) | data formatting | bytes 131072
  78.1 1.5 %copy.12 = f32[32,512]{1,0:T(8,128)} copy(f32[32,512]{1,0:T(8,128)} %get-tuple-element.7) | data formatting | bytes 131072
  79.6 1.4 %copy.13 = f32[2,32,32]{2,1,0:T(8,128)} copy(f32[2,32,32]{2,1,0:T(8,128)} %get-tuple-element.8) | data formatting | bytes 16384

commit v6 on v4

--- a/solution.py
+++ b/solution.py
@@ -18,7 +18,7 @@
     return high, (a - high.astype(f32)).astype(bf16)
 
 
-PIECES = 2
+PIECES = 4
 
 
 def dot(a, b, dims):

time: 78.2 us -> 76.3 us (0.976)
  Pallas kernels: 73 us -> 71.1 us
    pallas_call x1, Pallas kernels: 73 us -> 71.1 us  [shards(): pl.pallas_call(functools.partial(kernel, n), out_shape=(jax.ShapeDtypeStr...]
where the time goes in v6:
time: 76.3 us; the launch traced here: 76.1 us
  Pallas kernels  71.1 us (93%)
  local copies, waits for them, and re-layouts  4.32 us (6%)
    pallas_call x1, Pallas kernels, shards(): pl.pallas_call(functools.partial(kernel, n), out_shape=(jax.ShapeDtypeStr...  71.1 us
    unnamed x3, local copies, waits for them, and re-layouts  4.32 us

profile of v6, /device:TPU:0, one launch (start us, length us, event | category | flops | bytes accessed | tf_op | source)
XLA Modules:
  0.0 76.1 jit_solution(10759870254977401658)
XLA Ops:
  0.6 71.1 %filter_pass.1 = (f32[32,512]{1,0:T(8,128)}, f32[32,512]{1,0:T(8,128)}, f32[2,32,32]{2,1,0:T(8,128)}) custom-call(f32[32,512]{1,0:T(8,128)} %f_hbm.1, f32[4,2,512,256]{3,2,1,0:T(8,128)} %bitcast.2, f32[2,256,256]{2,1,0:T(8,128)} %e_hbm.1, f32[2,256,256]{2,1,0:T(8,128)} %d_hbm.1, f32[2,4]{1,0:T(2,128)} %bitcast.3), custom_call_target="tpu_custom_call" | custom-call | tf_op jit(solution)/shard_map/filter_pass/pallas_call | solution.py:504
  71.7 1.5 %copy.11 = f32[32,512]{1,0:T(8,128)} copy(f32[32,512]{1,0:T(8,128)} %get-tuple-element.6) | data formatting | bytes 131072
  73.2 1.5 %copy.12 = f32[32,512]{1,0:T(8,128)} copy(f32[32,512]{1,0:T(8,128)} %get-tuple-element.7) | data formatting | bytes 131072
  74.7 1.4 %copy.13 = f32[2,32,32]{2,1,0:T(8,128)} copy(f32[2,32,32]{2,1,0:T(8,128)} %get-tuple-element.8) | data formatting | bytes 16384
